TPU v7x, 128 devices: a whole 4x4x4 slice. The times are simulated.
128 devices in a mesh: section: 2 (over y_hi), dp: 4 (over x), seq: 16 (over z, y_lo, core).
Axes of the slice: x: 4, y: 4 (y_hi: 2, y_lo: 2; y = y_hi * 2 + y_lo), z: 4, core: 2. Of those that a mesh axis runs over, the one named last changes fastest.
Arguments:
- trajectory: bfloat16 [5, 4, 16, 128, 128], P(None, None, 'seq', 'dp'), may hold values from -12 to 12
- block_input: bfloat16 [4, 4096, 3072], P('dp', 'seq'), may hold values from -6 to 6
- chosen: int32 [4], replicated, may hold values from 0 to 3
- lengths: int32 [4], replicated, may hold values from 1024 to 4096, as said below
- rewards: int32 [64], replicated, may hold values from 0 to 9
- prompt_group_index: int32 [64], replicated, may hold values from 0 to 3, as said below
- rollout_log_probability: float32 [4], replicated, may hold values from -0.95 to -0.5
- timestep_norm_shift: float32 [4, 2, 3072], replicated, may hold values from -2.5 to 2.5
- patch_input_weight: bfloat16 [64, 3072], replicated, may hold values from -0.75 to 0.75
- frozen_query_matrix: bfloat16 [3072, 1536], P(None, 'section'), may hold values from -1 to 1
- frozen_key_matrix: bfloat16 [3072, 1536], P(None, 'section'), may hold values from -1 to 1
- frozen_value_matrix: bfloat16 [3072, 1536], P(None, 'section'), may hold values from -0.109375 to 0.109375
- velocity_output_weight: bfloat16 [1536, 64], P('section'), may hold values from -0.15625 to 0.15625
- adapter_down_factor: float32 [3072, 128], replicated, may hold values from -6 to 6
- adapter_up_factor: float32 [128, 1536], P(None, 'section'), may hold values from -6 to 6
Outputs:
- revised_down_factor: float32 [3072, 128], replicated
- revised_up_factor: float32 [128, 1536], P(None, 'section')
- ratios: float32 [4], P('dp')
Inputs may be any that keep to these rules, and one draw needn't show every extreme that they name: `lengths`: the longest trained clip has all 4096 tokens live. `prompt_group_index`: each of the 4 prompts names exactly 16 clips.
All inputs are finite; a program needn't handle non-finite values.
Results may differ from a plain program's by a relative error of at most 0.015.
Values may be sent and summed in bfloat16 or wider, within the bound.
A program may use at most 192 MiB of HBM per device.

v0:
```python
import math

import jax
import jax.numpy as jnp
from jax import lax
from jax.sharding import PartitionSpec as P

MODEL_WIDTH = 3072
HD = 128
ADAPTER_RANK = 128
STEPS = 4
GROUP = 16
GROUPS = 4


noise_level = 0.8
clip_range = 0.2
step_length = 256.0
norm_eps = 1e-06
masked_score = -1e30


def advantages(rewards, prompt_group_index):
    member = (prompt_group_index[:, None] == jnp.arange(GROUPS)[None, :]).astype(jnp.float32)
    reward_values = rewards.astype(jnp.float32)
    group_mean = jnp.sum(member * reward_values[:, None], axis=0) / GROUP
    own_mean = jnp.sum(member * group_mean[None, :], axis=1)
    centered = reward_values - own_mean
    group_var = jnp.sum(member * (centered * centered)[:, None], axis=0) / GROUP
    own_std = jnp.sum(member * jnp.sqrt(group_var)[None, :], axis=1)
    return centered / (own_std + 1.0)


def clip_weight(advantage, ratios, clip_total):
    low_edge = 1.0 - clip_range
    high_edge = 1.0 + clip_range
    inside = (ratios >= low_edge) & (ratios <= high_edge)
    active = inside | (advantage > 0) & (ratios < low_edge) | (advantage < 0) & (ratios > high_edge)
    return jnp.where(active, -advantage * ratios / clip_total, 0.0)


def split_rows(rows, head_count):
    return rows.reshape(rows.shape[0], rows.shape[1], head_count, HD)


def key_scores(queries, key_heads, live_len):
    scores = jnp.einsum(
        "cqhd,ckhd->chqk", queries, key_heads, preferred_element_type=jnp.float32
    ) * (1.0 / math.sqrt(HD))
    positions = jnp.arange(key_heads.shape[1])
    live_mask = (positions[None, :] < live_len[:, None])[:, None, None, :]
    return (jnp.where(live_mask, scores, masked_score), live_mask)


def attend_block(running, key_rows, value_rows, queries, live_len):
    maxima, totals, accumulated = running
    key_heads = split_rows(key_rows, queries.shape[2])
    value_heads = split_rows(value_rows, queries.shape[2])
    scores, live_mask = key_scores(queries, key_heads, live_len)
    new_max = jnp.maximum(maxima, jnp.max(scores, axis=3))
    exp_scores = jnp.where(live_mask, jnp.exp(scores - new_max[..., None]), 0.0)
    totals = jnp.sum(exp_scores, axis=3)
    weighted = jnp.einsum(
        "chqk,ckhd->cqhd",
        exp_scores.astype(jnp.bfloat16),
        value_heads,
        preferred_element_type=jnp.float32,
    )
    accumulated = weighted
    return (new_max, totals, accumulated)


def return_block(key_rows, value_rows, queries, live_len, grad_out, deltas, maxima, totals):
    key_heads = split_rows(key_rows, queries.shape[2])
    value_heads = split_rows(value_rows, queries.shape[2])
    scores, live_mask = key_scores(queries, key_heads, live_len)
    probabilities = jnp.where(
        live_mask, jnp.exp(scores - maxima[..., None]) / totals[..., None], 0.0
    )
    grad_probs = jnp.einsum(
        "cqhd,ckhd->chqk", grad_out, value_heads, preferred_element_type=jnp.float32
    )
    grad_scores = (probabilities * (grad_probs - deltas[..., None])).astype(jnp.bfloat16)
    return jnp.einsum("chqk,ckhd->cqhd", grad_scores, key_heads, preferred_element_type=jnp.float32)


def shards(
    trajectory,
    block_input,
    chosen,
    lengths,
    rewards,
    prompt_group_index,
    rollout_log_probability,
    timestep_norm_shift,
    patch_input_weight,
    frozen_query_matrix,
    frozen_key_matrix,
    frozen_value_matrix,
    velocity_output_weight,
    adapter_down_factor,
    adapter_up_factor,
):
    dp_count = lax.axis_size("dp")
    dp_index = lax.axis_index("dp")
    seq_index = lax.axis_index("seq")
    clip_count = chosen.shape[0]
    own_clips = clip_count // dp_count
    first_clip = dp_index * own_clips
    levels = jnp.arange(trajectory.shape[0])
    pick_now = (levels[:, None] == chosen[None, :])[:, :, None, None, None]
    pick_next = (levels[:, None] == chosen[None, :] + 1)[:, :, None, None, None]
    zero_frame = jnp.zeros((), trajectory.dtype)
    current_all = jnp.sum(jnp.where(pick_now, trajectory, zero_frame), axis=0)
    next_all = jnp.sum(jnp.where(pick_next, trajectory, zero_frame), axis=0)
    current, following = (
        lax.all_to_all(current_all, "dp", split_axis=0, concat_axis=2, tiled=True),
        lax.all_to_all(next_all, "dp", split_axis=0, concat_axis=2, tiled=True),
    )
    tok_local = current.shape[2] * 2
    patch_width = current.shape[3] // 2
    current = current.reshape(own_clips, tok_local, patch_width)
    following = following.reshape(own_clips, tok_local, patch_width)
    my_chosen = lax.dynamic_slice_in_dim(chosen, first_clip, own_clips)
    my_lengths = lax.dynamic_slice_in_dim(lengths, first_clip, own_clips)
    my_old = lax.dynamic_slice_in_dim(rollout_log_probability, first_clip, own_clips)
    step_size = 1.0 / (STEPS + 1)
    noise_sigma = 1.0 - my_chosen.astype(jnp.float32) * step_size
    spread = noise_level * jnp.sqrt(step_size * noise_sigma)
    pick_mod = (jnp.arange(STEPS)[None, :] == my_chosen[:, None])[:, :, None, None]
    modulation = jnp.sum(jnp.where(pick_mod, timestep_norm_shift[None], 0.0), axis=1)
    embedded = block_input.astype(jnp.float32) + jnp.dot(
        current, patch_input_weight, preferred_element_type=jnp.float32
    )
    normed = embedded / jnp.sqrt(jnp.mean(embedded * embedded, axis=2, keepdims=True) + norm_eps)
    normalized_input = (
        normed * (1.0 + modulation[:, 1][:, None, :]) + modulation[:, 0][:, None, :]
    ).astype(jnp.bfloat16)
    input_scale = 1.0 / math.sqrt(MODEL_WIDTH)
    out_scale = 1.0 / math.sqrt(ADAPTER_RANK)
    narrow_query_part = (
        jnp.dot(
            normalized_input,
            adapter_down_factor.astype(jnp.bfloat16),
            preferred_element_type=jnp.float32,
        )
        * input_scale
    ).astype(jnp.bfloat16)
    upper_adapter_half = adapter_up_factor.astype(jnp.bfloat16)
    query_proj = (
        jnp.dot(normalized_input, frozen_query_matrix, preferred_element_type=jnp.float32)
        + jnp.dot(narrow_query_part, upper_adapter_half, preferred_element_type=jnp.float32)
        * out_scale
    ).astype(jnp.bfloat16)
    key_proj = jnp.dot(
        normalized_input, frozen_key_matrix, preferred_element_type=jnp.float32
    ).astype(jnp.bfloat16)
    value_proj = jnp.dot(
        normalized_input, frozen_value_matrix, preferred_element_type=jnp.float32
    ).astype(jnp.bfloat16)
    heads_loc = frozen_query_matrix.shape[1] // HD
    queries = split_rows(query_proj, heads_loc)
    start_state = (
        jnp.full((own_clips, heads_loc, tok_local), masked_score, jnp.float32),
        jnp.zeros((own_clips, heads_loc, tok_local), jnp.float32),
        jnp.zeros((own_clips, tok_local, heads_loc, HD), jnp.float32),
    )
    pieces = (
        lax.all_gather(key_proj, "seq", axis=1, tiled=True),
        lax.all_gather(value_proj, "seq", axis=1, tiled=True),
    )
    running = attend_block(start_state, pieces[0], pieces[1], queries, my_lengths)
    maxima, totals, accumulated = running
    attn_heads = (accumulated / jnp.transpose(totals, (0, 2, 1))[..., None]).astype(jnp.bfloat16)
    attn_out = attn_heads.reshape(own_clips, tok_local, heads_loc * HD)
    velocity = lax.psum(
        jnp.dot(attn_out, velocity_output_weight, preferred_element_type=jnp.float32).astype(
            jnp.bfloat16
        ),
        "section",
    ).astype(jnp.float32)
    positions = seq_index * tok_local + jnp.arange(tok_local)
    live_tokens = positions[None, :] < my_lengths[:, None]
    zscore = (
        following.astype(jnp.float32) - current.astype(jnp.float32) + step_size * velocity
    ) / spread[:, None, None]
    counts = (my_lengths * patch_width).astype(jnp.float32)
    squares = jnp.where(live_tokens[:, :, None], zscore * zscore, 0.0)
    clip_squares = lax.psum(jnp.sum(squares, axis=(1, 2)), "seq")
    logprob = -0.5 * clip_squares / counts
    ratios = jnp.exp(logprob - my_old)
    advantage = lax.dynamic_slice_in_dim(
        advantages(rewards, prompt_group_index), first_clip, own_clips
    )
    weight = clip_weight(advantage, ratios, float(clip_count))
    grad_vel = jnp.where(
        live_tokens[:, :, None],
        -weight[:, None, None]
        * zscore
        * step_size
        / (spread[:, None, None] * counts[:, None, None]),
        0.0,
    ).astype(jnp.bfloat16)
    grad_out = jnp.dot(
        grad_vel, velocity_output_weight.T, preferred_element_type=jnp.float32
    ).astype(jnp.bfloat16)
    grad_heads = split_rows(grad_out, heads_loc)
    deltas = jnp.transpose(
        jnp.sum(grad_heads.astype(jnp.float32) * attn_heads.astype(jnp.float32), axis=3), (0, 2, 1)
    )
    pieces = (
        lax.all_gather(key_proj, "seq", axis=1, tiled=True),
        lax.all_gather(value_proj, "seq", axis=1, tiled=True),
    )
    grad_sum = return_block(
        pieces[0], pieces[1], queries, my_lengths, grad_heads, deltas, maxima, totals
    )
    grad_q = (
        (grad_sum * (1.0 / math.sqrt(HD)))
        .astype(jnp.bfloat16)
        .reshape(own_clips * tok_local, heads_loc * HD)
    )
    low_rows = narrow_query_part.reshape(own_clips * tok_local, ADAPTER_RANK)
    up_term = (
        lax.dot_general(
            low_rows, grad_q, (((0,), (0,)), ((), ())), preferred_element_type=jnp.float32
        )
        * out_scale
    )
    low_partial = (
        jnp.dot(grad_q, upper_adapter_half.T, preferred_element_type=jnp.float32) * out_scale
    )
    grad_low = lax.psum(low_partial.astype(jnp.bfloat16), "section")
    normed_rows = normalized_input.reshape(own_clips * tok_local, MODEL_WIDTH)
    down_term = (
        lax.dot_general(
            normed_rows, grad_low, (((0,), (0,)), ((), ())), preferred_element_type=jnp.float32
        )
        * input_scale
    )
    down_gradient = lax.psum(down_term, ("dp", "seq"))
    up_gradient = lax.psum(up_term, ("dp", "seq"))
    update_factor = step_length / jnp.sqrt(jnp.sum(down_gradient * down_gradient) + norm_eps)
    revised_down_factor = adapter_down_factor - update_factor * down_gradient
    revised_up_factor = adapter_up_factor - update_factor * up_gradient
    return (revised_down_factor, revised_up_factor, ratios)


def solution(mesh):
    return jax.shard_map(
        shards,
        mesh=mesh,
        in_specs=(
            P(None, None, "seq", "dp", None),
            P("dp", "seq", None),
            P(),
            P(),
            P(),
            P(),
            P(),
            P(),
            P(),
            P(None, "section"),
            P(None, "section"),
            P(None, "section"),
            P("section", None),
            P(),
            P(None, "section"),
        ),
        out_specs=(P(), P(None, "section"), P("dp")),
        check_vma=False,
    )
```

profile of v0, /device:TPU:1, one launch (start us, length us, event | category | flops | bytes accessed | tf_op | source)
XLA Modules:
  0.0 798.7 jit_solution(1844641214466060099)
XLA Ops:
  7.2 0.7 broadcast_add_fusion
  7.9 0.7 iota_compare_fusion.1
  8.6 1.7 select_reduce_fusion.1
  10.2 4.8 all-to-all-start
  15.1 1.2 dynamic_slice.12
  16.3 0.6 iota_compare_fusion.4
  17.0 1.0 select_reduce_fusion.3
  18.0 1.4 all-to-all-done
  19.5 2.2 multiply_reduce_fusion
  22.3 2.2 fusion.18
  24.6 4.6 fusion.21
  29.2 4.0 all-to-all-start.1
  33.4 0.7 dynamic_slice.13
  34.1 0.7 iota_compare_fusion
  35.3 0.7 add_compare_fusion
  36.6 0.6 dynamic_slice.15
  39.2 1.2 dynamic_slice.14
  41.2 1.4 convert_subtract_fusion
  42.6 1.6 sub.56
  44.1 1.6 copy.46
  45.8 0.6 fusion.29
  46.3 3.9 fusion.10
  50.2 1.0 fusion.17
  51.2 1.9 copy.42
  53.1 16.3 %all-gather.5.cloned.1.call-done = bf16[4096,768]{1,0:T(8,128)(2,1)} async-done(((bf16[256,768]{1,0:T(8,128)(2,1)}), bf16[4096,768]{1,0:T(8,128)(2,1)}) %all-gather.5.cloned.1.call-update) | async-done | bytes 6291472 | tf_op jit(solution)/shard_map/all_gather | solution.py:212
  69.5 8.7 %copy.41 = bf16[4096,768]{0,1:T(8,128)(2,1)} copy(bf16[4096,768]{1,0:T(8,128)(2,1)} %all-gather.5.cloned.1.call-done) | data formatting | bytes 12582912 | tf_op jit(solution)/shard_map/all_gather | solution.py:212
  78.2 16.0 %fusion = (f32[6,256]{1,0:T(8,128)S(1)}, f32[6,256,4096]{2,1,0:T(8,128)}) fusion(pred[4096]{0:T(1024)(128)(4,1)S(1)} %iota_compare_fusion, bf16[256,6,128]{0,2,1:T(8,128)(2,1)} %bitcast.104, bf16[4096,6,128]{0,2,1:T(8,128)(2,1)} %bitcast.99), kind=kOutput, calls=%fused_computation.5 | convolution fusion | flops 1629485568 | bytes 31860736 | tf_op jit(solution)/shard_map/cqhd,ckhd->chqk/dot_general | solution.py:47
  94.2 12.9 %select_reduce_fusion = f32[6,256]{1,0:T(8,128)} fusion(f32[6,256,4096]{2,1,0:T(8,128)} %get-tuple-element.12, f32[6,256]{1,0:T(8,128)S(1)} %broadcast_maximum_fusion, pred[4096]{0:T(1024)(128)(4,1)S(1)} %iota_compare_fusion), kind=kLoop, calls=%fused_computation.4 | loop fusion | flops 31455744 | bytes 25182208 | tf_op jit(solution)/shard_map/reduce_sum | solution.py:62
  107.1 7.4 all-gather.7.cloned.1.call-done
  114.5 8.6 %copy.45 = bf16[4096,768]{0,1:T(8,128)(2,1)} copy(bf16[4096,768]{1,0:T(8,128)(2,1)} %all-gather.7.cloned.1.call-done) | data formatting | bytes 12582912 | tf_op jit(solution)/shard_map/all_gather | solution.py:170
  123.1 14.2 %fusion.34 = bf16[1,256,6,128]{1,3,2,0:T(8,128)(2,1)} fusion(bf16[4096,6,128]{0,2,1:T(8,128)(2,1)} %bitcast.101, f32[6,256,4096]{2,1,0:T(8,128)} %get-tuple-element.12, f32[6,256]{1,0:T(8,128)S(1)} %broadcast_maximum_fusion, pred[4096]{0:T(1024)(128)(4,1)S(1)} %iota_compare_fusion, f32[256,6]{0,1:T(8,128)} %bitcast.113), kind=kOutput, calls=%fused_computation.42 | convolution fusion | flops 1642463232 | bytes 31866880 | tf_op jit(solution)/shard_map/chqk,ckhd->cqhd/dot_general | solution.py:63
  137.3 1.9 fusion.32
  139.1 10.4 %psum.35 = bf16[1,256,64]{1,2,0:T(8,128)(2,1)} all-reduce(bf16[1,256,64]{1,2,0:T(8,128)(2,1)} %fusion.32), channel_id=1, replica_groups=mesh['section'=2,'dp'=4,'seq'=16] {'section'}, use_global_device_ids=true, to_apply=%region_6.7 | all-reduce | flops 16384 | bytes 65536 | tf_op jit(solution)/shard_map/psum | solution.py:176
  149.6 1.5 select_reduce_fusion.4
  151.0 29.6 %psum.36 = f32[1]{0:T(128)} all-reduce(f32[1]{0:T(128)} %bitcast.20), channel_id=1, replica_groups=mesh['section'=2,'dp'=4,'seq'=16] {'seq'}, use_global_device_ids=true, to_apply=%region_8.9 | all-reduce | flops 1 | bytes 8 | tf_op jit(solution)/shard_map/psum | solution.py:189
  182.0 2.0 convolution_convert_fusion
  184.0 2.0 copy.47
  186.0 2.0 copy.50
  188.0 1.9 multiply_reduce_fusion.2
  189.9 18.4 %fusion.24 = bf16[6,128,256]{2,1,0:T(8,128)(2,1)} fusion(bf16[4096,6,128]{0,2,1:T(8,128)(2,1)} %bitcast.100, f32[6,256,4096]{2,1,0:T(8,128)} %get-tuple-element.12, f32[6,256]{1,0:T(8,128)} %bitcast.114, f32[6,256]{1,0:T(8,128)} %select_reduce_fusion, f32[6,256]{1,0:T(8,128)S(1)} %broadcast_maximum_fusion, pred[4096]{0:T(1024)(128)(4,1)S(1)} %iota_compare_fusion, ...), kind=kOutput, calls=%fused_computation.33 | convolution fusion | flops 3271950336 | bytes 38557696 | tf_op jit(solution)/shard_map/chqk,ckhd->cqhd/dot_general | solution.py:84
  208.4 1.9 fusion.28
  210.4 2.1 convolution_multiply_fusion.2
  212.5 24.1 %all-reduce.4.cloned.1.call-done = bf16[256,128]{1,0:T(8,128)(2,1)} async-done(((bf16[256,128]{1,0:T(8,128)(2,1)}), bf16[256,128]{1,0:T(8,128)(2,1)}) %all-reduce.4.cloned.1.call-update) | async-done | bytes 65552 | tf_op jit(solution)/shard_map/psum | solution.py:233
  236.6 2.6 convolution_multiply_fusion
  239.2 545.2 %all-reduce.6.cloned.1.call-done = (f32[3072,128]{1,0:T(8,128)}, f32[128,768]{1,0:T(8,128)}) async-done(((f32[3072,128]{1,0:T(8,128)}, f32[128,768]{1,0:T(8,128)}), (f32[3072,128]{1,0:T(8,128)}, f32[128,768]{1,0:T(8,128)})) %all-reduce.6.cloned.1.call-update) | async-done | bytes 1966096 | tf_op jit(solution)/shard_map/psum | solution.py:241
  784.4 2.5 multiply_reduce_fusion.1
  787.6 2.7 multiply_subtract_fusion
  790.3 0.8 multiply_subtract_fusion.1
  (47 shorter events, 1.6 us)
Async XLA Ops:
  7.2 12.3 %copy-start = (bf16[64,3072]{1,0:T(8,128)(2,1)S(1)}, bf16[64,3072]{1,0:T(8,128)(2,1)}, u32[]{:S(2)}) copy-start(bf16[64,3072]{1,0:T(8,128)(2,1)} %param.23) | copy-start | bytes 1179652
  10.2 9.1 %all-to-all-start = ((bf16[4,1,32,128]{3,2,1,0:T(8,128)(2,1)}), bf16[4,1,32,128]{3,2,1,0:T(8,128)(2,1)S(1)}, u32[]{:S(2)}, u32[]{:S(2)}) async-start(bf16[4,1,32,128]{3,2,1,0:T(8,128)(2,1)} %bitcast), calls=%async_computation | async-start | bytes 65536 | tf_op jit(solution)/shard_map/all_to_all | solution.py:117
  15.1 54.4 %all-gather.5.cloned.1.call-start = ((), (), s32[]{:S(2)}) async-start(), calls=%async_computation.3 | async-start | bytes 6684672 | tf_op jit(solution)/shard_map/all_gather | solution.py:212
  19.4 2.3 copy-start.7
  19.5 2.8 copy-start.9
  24.5 9.0 %copy-start.10 = (s32[4]{0:T(128)S(1)}, s32[4]{0:T(128)}, u32[]{:S(2)}) copy-start(s32[4]{0:T(128)} %param.18) | copy-start | bytes 52
  24.5 9.6 %copy-start.8 = (s32[64]{0:T(128)S(1)}, s32[64]{0:T(128)}, u32[]{:S(2)}) copy-start(s32[64]{0:T(128)} %param.19) | copy-start | bytes 772
  24.5 10.3 %copy-start.11 = (s32[64]{0:T(128)S(1)}, s32[64]{0:T(128)}, u32[]{:S(2)}) copy-start(s32[64]{0:T(128)} %param.20) | copy-start | bytes 772
  24.5 21.3 %copy-start.2 = (f32[3072,128]{1,0:T(8,128)S(1)}, f32[3072,128]{1,0:T(8,128)}, u32[]{:S(2)}) copy-start(f32[3072,128]{1,0:T(8,128)} %param.28) | copy-start | bytes 4718596
  24.5 90.0 %all-gather.7.cloned.1.call-start = ((), (), s32[]{:S(2)}) async-start(), calls=%async_computation.4 | async-start | bytes 6684672 | tf_op jit(solution)/shard_map/all_gather | solution.py:170
  29.2 21.0 %copy-start.3 = (f32[128,768]{1,0:T(8,128)S(1)}, f32[128,768]{1,0:T(8,128)}, u32[]{:S(2)}) copy-start(f32[128,768]{1,0:T(8,128)} %param.29) | copy-start | bytes 1179652
  29.2 12.0 %all-to-all-start.1 = ((bf16[4,1,32,128]{3,2,1,0:T(8,128)(2,1)}), bf16[4,1,32,128]{3,2,1,0:T(8,128)(2,1)}, u32[]{:S(2)}, u32[]{:S(2)}) async-start(bf16[4,1,32,128]{3,2,1,0:T(8,128)(2,1)} %bitcast.109), calls=%async_computation.1 | async-start | bytes 65536 | tf_op jit(solution)/shard_map/all_to_all | solution.py:118
  33.2 203.4 %all-reduce.4.cloned.1.call-start = ((), (), s32[]{:S(2)}) async-start(), calls=%async_computation.2 | async-start | bytes 131072 | tf_op jit(solution)/shard_map/psum | solution.py:233
  46.3 3.9 copy-start.5
  210.3 574.1 %all-reduce.6.cloned.1.call-start = ((), (), s32[]{:S(2)}) async-start(), calls=%async_computation.5 | async-start | bytes 3932160 | tf_op jit(solution)/shard_map/psum | solution.py:241
  210.4 580.7 %copy-start.1 = (bf16[64,3072]{1,0:T(8,128)(2,1)S(1)}, bf16[64,3072]{1,0:T(8,128)(2,1)}, u32[]{:S(2)}) copy-start(bf16[64,3072]{1,0:T(8,128)(2,1)} %param.23) | copy-start | bytes 1179652
  239.2 551.1 %copy-start.4 = (f32[128,768]{1,0:T(8,128)S(1)}, f32[128,768]{1,0:T(8,128)}, u32[]{:S(2)}) copy-start(f32[128,768]{1,0:T(8,128)} %param.29) | copy-start | bytes 1179652
  784.4 5.9 copy-start.6
Sparse Core Ops, SparseCore 0:
  24.6 44.7 all-gather.4
  71.2 43.2 all-gather.6
  210.4 26.0 all-reduce.3
  239.6 544.8 all-reduce.5
where the time goes:
time: 803 us; the launch traced here: 799 us
  waiting for transfers between devices  594 us (74%)
  matrix products  73.6 us (9%)
  blocking collectives  40.1 us (5%)
  other arithmetic  30.8 us (4%)
  local copies, waits for them, and re-layouts  30.4 us (4%)
  between operations  20.4 us (3%)
  starting transfers between devices  9.16 us (1%)
    psum x1, waiting for transfers between devices, shards(): down_gradient = lax.psum(down_term, ('dp', 'seq'))  545 us
    psum x1, blocking collectives, shards(): clip_squares = lax.psum(jnp.sum(squares, axis=(1, 2)), 'seq')  29.6 us
    psum x1, waiting for transfers between devices, shards(): grad_low = lax.psum(low_partial.astype(jnp.bfloat16), 'section')  24.1 us
    dot_general x1, matrix products, return_block(): jnp.einsum('chqk,ckhd->cqhd', grad_scores, key_heads, preferred_element_t...  18.4 us
    all_gather x1, waiting for transfers between devices, shards(): lax.all_gather(key_proj, 'seq', axis=1, tiled=True)  16.3 us
  transfers between devices with their start and end apart: 6, of which 5 were waited for; matrix products, arithmetic and copies ran while one was open for 8% of the time, Pallas kernels for 0%

commit v1 on v0

v1 whole, which is shorter than its diff:
```python
import functools
import math

import jax
import jax.numpy as jnp
from jax import lax
from jax.experimental import pallas as pl
from jax.experimental.pallas import tpu as pltpu
from jax.sharding import PartitionSpec as P

MESH = pl.DeviceIdType.MESH
F32 = jnp.float32
BF16 = jnp.bfloat16

MODEL_WIDTH = 3072
HD = 128
ADAPTER_RANK = 128
STEPS = 4
GROUP = 16
PATCH = 64
CLIPS = 4
ROWS = 256
PAIRS = 32
OWN = 384
PLANE = 1024
HALF = 1536

noise_level = 0.8
clip_range = 0.2
step_length = 256.0
norm_eps = 1e-06
masked_score = -1e30
step_size = 1.0 / (STEPS + 1)
input_scale = 1.0 / math.sqrt(MODEL_WIDTH)
out_scale = 1.0 / math.sqrt(ADAPTER_RANK)
head_scale = 1.0 / math.sqrt(HD)
query_scale = head_scale * math.log2(math.e)

NT = (((1,), (1,)), ((), ()))

R_X = 0
R_PAIR = 3
R_Z = 8
R_FAR = 16
R_CORE = 20
R_VEL = 36
R_SQ = 39
R_LOW = 46
R_RC = 49
R_RX = 50
R_RZ = 53
R_RY = 56
R_GZ = 59
R_GX = 62
R_GC = 65
N_RECV = 69
N_SEND = 96


def dot(a, b):
    return jnp.dot(a, b, preferred_element_type=F32)


def dot_nt(a, b):
    return lax.dot_general(a, b, NT, preferred_element_type=F32)


def iota(shape, dim):
    return lax.broadcasted_iota(jnp.int32, shape, dim)


def lanes(start, size):
    return pl.ds(pl.multiple_of(start, 128), size)


def rows_at(start, size, unit=256):
    return pl.ds(pl.multiple_of(start, unit), size)


def body(
    chosen_ref, lengths_ref, rollout_ref,
    traj_ref, rewards_ref, groups_ref, shift_ref, patch_ref, wout_ref, down_ref, up_ref,
    x_hbm, wq_hbm, wk_hbm, wv_hbm,
    out_down, out_up, out_ratio,
    xin, wq, wk, wv, downb, upb, emb, normed,
    sel, latents, stage_k, stage_v, stage_q, keys, values, queries, low,
    top, total, acc, attn, vel, squares, gout, gq, glow_send, glow,
    du, core_recv, xs, xr, zs, zr, yr, zg, full,
    send_sem, recv_sem, local_sem,
):
    sec = lax.axis_index("section")
    x = lax.axis_index("dp")
    seq = lax.axis_index("seq")
    z = seq // 4
    yl = (seq // 2) % 2
    core = seq % 2
    y = sec * 2 + yl

    def at(sec_, x_, z_, yl_, core_):
        return (sec_, x_, z_ * 4 + yl_ * 2 + core_)

    def y_peer(step):
        other = (y + step) % 4
        return other, at(other // 2, x, z, other % 2, core)

    other_core = at(sec, x, z, yl, 1 - core)
    partner = at(sec, x, z, 1 - yl, core)
    z_up = at(sec, x, (z + 1) % 4, yl, core)
    z_down = at(sec, x, (z + 3) % 4, yl, core)

    pending = []

    def descriptor(src, dst, send_index, recv_index, device):
        return pltpu.make_async_remote_copy(
            src_ref=src, dst_ref=dst, send_sem=send_sem.at[send_index], recv_sem=recv_sem.at[recv_index],
            device_id=device, device_id_type=MESH,
        )

    def send(src, dst, recv_index, device):
        copy = descriptor(src, dst, len(pending), recv_index, device)
        copy.start()
        pending.append(copy)

    def arrive(dst, recv_index):
        descriptor(dst, dst, 0, recv_index, other_core).wait_recv()

    loads = []

    def load(src, dst):
        copy = pltpu.make_async_copy(src, dst, local_sem.at[len(loads)])
        copy.start()
        loads.append(copy)
        return copy

    load_x = load(x_hbm, xin)
    own_cols, other_cols = lanes(yl * OWN, OWN), lanes((1 - yl) * OWN, OWN)
    load_w = []
    for src, dst in ((wk_hbm, wk), (wv_hbm, wv), (wq_hbm, wq)):
        load_w.append((load(src.at[:, own_cols], dst.at[:, 0:OWN]), load(src.at[:, other_cols], dst.at[:, OWN : 2 * OWN])))

    peers = [at(sec, (x + d) % 4, z, yl, core) for d in (1, 2, 3)]
    peers += [y_peer(d)[1] for d in (1, 2, 3)]
    peers += [at(sec, x, (z + d) % 4, yl, core) for d in (1, 2, 3)]
    peers += [at(sec, x, (z + d) % 4, yl, 1 - core) for d in (0, 1, 2, 3)]
    barrier = pltpu.get_barrier_semaphore()
    for peer in peers:
        pl.semaphore_signal(barrier, inc=1, device_id=peer, device_id_type=MESH)

    for c in range(CLIPS):
        sel[c, 0] = traj_ref[chosen_ref[c], c]
        sel[c, 1] = traj_ref[chosen_ref[c] + 1, c]
    pl.semaphore_wait(barrier, len(peers))
    x_rows = rows_at(x * PAIRS, PAIRS, PAIRS)
    for d in (1, 2, 3):
        to = (x + d) % 4
        send(sel.at[to], latents.at[yl, :, x_rows, :], R_X + d - 1, at(sec, to, z, yl, core))
    latents[yl, :, x_rows, :] = sel[x]

    downb[...] = down_ref[...].astype(BF16)
    upb[:, 0:OWN] = up_ref[:, own_cols].astype(BF16)
    upb[:, OWN : 2 * OWN] = up_ref[:, other_cols].astype(BF16)

    chosen = chosen_ref[x]
    length = lengths_ref[x]
    one = jnp.ones((1, 1), F32)
    spread = noise_level * jnp.sqrt(step_size * (1.0 - one * chosen.astype(F32) * step_size))
    count = one * (length * PATCH).astype(F32)

    expand = jnp.where((iota((ROWS, 128), 0) >> 1) == iota((ROWS, 128), 1), 1.0, 0.0).astype(BF16)
    own_half = (iota((ROWS, 128), 1) >> 6) == (iota((ROWS, 128), 0) & 1)

    def token_rows(pairs):
        return jnp.where(own_half, dot(expand, pairs), 0.0).astype(BF16)

    def fold(offset, width):
        source = (iota((128, width), 0) & 63) + offset
        return jnp.where(source == iota((128, width), 1), 1.0, 0.0).astype(BF16)

    for d in (1, 2, 3):
        src_rows = rows_at(((x + 4 - d) % 4) * PAIRS, PAIRS, PAIRS)
        arrive(latents.at[yl, :, src_rows, :], R_X + d - 1)
    send(latents.at[yl], latents.at[yl], R_PAIR + 4, partner)

    now_tokens = dot(token_rows(latents[yl, 0]), fold(0, 64)).astype(BF16)
    load_x.wait()
    squares_sum = jnp.zeros((ROWS, 1), F32)
    chunk = 512
    for j in range(MODEL_WIDTH // chunk):
        cols = slice(j * chunk, (j + 1) * chunk)
        part = xin[:, cols].astype(F32) + dot(now_tokens, patch_ref[:, cols])
        emb[:, cols] = part
        squares_sum += jnp.sum(part * part, axis=1, keepdims=True)
    inverse = lax.rsqrt(squares_sum * (1.0 / MODEL_WIDTH) + norm_eps)
    for j in range(MODEL_WIDTH // chunk):
        cols = slice(j * chunk, (j + 1) * chunk)
        shift = shift_ref[chosen, 0:1, cols]
        scale = shift_ref[chosen, 1:2, cols]
        normed[:, cols] = (emb[:, cols] * inverse * (1.0 + scale) + shift).astype(BF16)

    seq_own = seq * ROWS
    seq_pair = (seq + 2 - 4 * yl) * ROWS

    def block(ref, z_, yl_, core_):
        return ref.at[rows_at((z_ * 4 + yl_ * 2 + core_) * ROWS, ROWS), :]

    def project(weight, loaded, stage, extra=None, scale=None):
        for copy in loaded:
            copy.wait()

        def step(n, carry):
            cols = lanes(n * 256, 256)
            part = dot(normed[...], weight[:, cols])
            if extra is not None:
                part = (part + dot(extra, upb[:, cols]) * out_scale) * scale
            stage[:, cols] = part.astype(BF16)
            return carry

        lax.fori_loop(0, 3, step, 0)

    store = (keys, values)

    def core_index(plane, pair, kv):
        return R_CORE + plane * 4 + pair * 2 + kv

    def to_core(plane, pair, kv):
        z_ = (z + plane) % 4
        yl_ = yl if pair == 0 else 1 - yl
        send(block(store[kv], z_, yl_, core), block(store[kv], z_, yl_, core), core_index(plane, pair, kv), other_core)

    def from_core(plane):
        z_ = (z + plane) % 4
        for pair in (0, 1):
            yl_ = yl if pair == 0 else 1 - yl
            for kv in (0, 1):
                arrive(block(store[kv], z_, yl_, 1 - core), core_index(plane, pair, kv))

    def z_index(pair, kv, above):
        return R_Z + pair * 4 + kv * 2 + above

    def to_z(pair, kv):
        src = block(store[kv], z, yl if pair == 0 else 1 - yl, core)
        send(src, src, z_index(pair, kv, 0), z_up)
        send(src, src, z_index(pair, kv, 1), z_down)

    def from_z(pair, kv, above):
        z_ = (z + 1) % 4 if above else (z + 3) % 4
        src = block(store[kv], z_, yl if pair == 0 else 1 - yl, core)
        arrive(src, z_index(pair, kv, above))
        if kv == 0 and not above:
            send(src, src, R_FAR + pair * 2 + kv, z_up)
        if kv == 1 and above:
            send(src, src, R_FAR + pair * 2 + kv, z_down)
        to_core(1 if above else 3, pair, kv)

    def from_far(pair, kv):
        arrive(block(store[kv], (z + 2) % 4, yl if pair == 0 else 1 - yl, core), R_FAR + pair * 2 + kv)
        to_core(2, pair, kv)

    own_block = rows_at(seq_own, ROWS)
    for kv, (weight, stage) in enumerate(((wk, stage_k), (wv, stage_v))):
        project(weight, load_w[kv], stage)
        send(stage.at[:, OWN : 2 * OWN], block(store[kv], z, yl, core), R_PAIR + kv, partner)
        store[kv][own_block, :] = stage[:, 0:OWN]
        to_z(0, kv)
        to_core(0, 0, kv)
    own_rows = rows_at(yl * ROWS, ROWS)
    pair_rows = rows_at((1 - yl) * ROWS, ROWS)
    low_own = (dot(normed[...], downb[...]) * input_scale).astype(BF16)
    low[own_rows, :] = low_own
    project(wq, load_w[2], stage_q, low_own, query_scale)
    send(stage_q.at[:, OWN : 2 * OWN], queries.at[own_rows, :], R_PAIR + 2, partner)
    queries[own_rows, :] = stage_q[:, 0:OWN]
    send(low.at[own_rows, :], low.at[own_rows, :], R_PAIR + 3, partner)
    for kv in (0, 1):
        arrive(block(store[kv], z, 1 - yl, core), R_PAIR + kv)
        to_z(1, kv)
        to_core(0, 1, kv)

    def key_bias(start):
        return jnp.where(start + iota((1, PLANE), 1) < length, 0.0, masked_score)

    def forward_plane(plane):
        start = ((z + plane) % 4) * PLANE
        plane_rows = rows_at(start, PLANE, PLANE)
        bias = key_bias(start)
        first = plane == 0

        def step(i, carry):
            head = i // 2
            cols = lanes(head * HD, HD)
            rows = rows_at((i % 2) * ROWS, ROWS)
            scores = dot_nt(queries[rows, cols], keys[plane_rows, cols]) + bias
            peak = jnp.max(scores, axis=1, keepdims=True)
            if not first:
                before = top[head, rows, :][:, 0:1]
                peak = jnp.maximum(peak, before)
            exp_scores = jnp.exp2(scores - peak)
            sums = jnp.sum(exp_scores, axis=1, keepdims=True)
            weighted = dot(exp_scores.astype(BF16), values[plane_rows, cols])
            if not first:
                decay = jnp.exp2(before - peak)
                sums += decay * total[head, rows, :][:, 0:1]
                weighted += decay * acc[rows, cols]
            top[head, rows, :] = jnp.broadcast_to(peak, (ROWS, 128))
            total[head, rows, :] = jnp.broadcast_to(sums, (ROWS, 128))
            acc[rows, cols] = weighted
            return carry

        lax.fori_loop(0, 6, step, 0)

    for kv in (0, 1):
        for above in (0, 1):
            from_z(0, kv, above)
    arrive(queries.at[pair_rows, :], R_PAIR + 2)
    from_core(0)
    forward_plane(0)
    for kv in (0, 1):
        for above in (0, 1):
            from_z(1, kv, above)
    from_core(1)
    forward_plane(1)
    from_far(0, 0)
    from_far(0, 1)
    from_core(3)
    forward_plane(3)
    from_far(1, 0)
    from_far(1, 1)
    from_core(2)
    forward_plane(2)

    def finish_head(i, carry):
        head = i // 2
        cols = lanes(head * HD, HD)
        rows = rows_at((i % 2) * ROWS, ROWS)
        sums = total[head, rows, :]
        attn[rows, cols] = (acc[rows, cols] / sums).astype(BF16)
        top[head, rows, :] = top[head, rows, :] + jnp.log(sums) * math.log2(math.e)
        return carry

    lax.fori_loop(0, 6, finish_head, 0)

    wout = wout_ref[rows_at(yl * OWN, OWN, 128), :]
    spread_cols = [
        jnp.where(iota((PATCH, 128), 0) + PATCH * b == iota((PATCH, 128), 1), 1.0, 0.0).astype(BF16) for b in (0, 1)
    ]
    wide = [dot(wout, cols).astype(BF16) for cols in spread_cols]
    partial = dot(attn[0:ROWS, :], wide[0]) + dot(attn[ROWS : 2 * ROWS, :], wide[1])
    vel[y] = partial.astype(BF16)
    for d in (1, 2, 3):
        send(vel.at[y], vel.at[y], R_VEL + d - 1, y_peer(d)[1])
    arrive(latents.at[1 - yl], R_PAIR + 4)
    arrive(low.at[pair_rows, :], R_PAIR + 3)
    moved = jnp.zeros((ROWS, 128), F32)
    for b in (0, 1):
        moved += dot(token_rows(latents[b, 1]), fold(PATCH * b, 128))
        moved -= dot(token_rows(latents[b, 0]), fold(PATCH * b, 128))
    lane_block = iota((ROWS, 128), 1) >> 6
    position = (z * 4 + lane_block * 2 + core) * ROWS + iota((ROWS, 128), 0)
    live = position < length
    for d in (1, 2, 3):
        arrive(vel.at[(y + 4 - d) % 4], R_VEL + d - 1)
    velocity = jnp.zeros((ROWS, 128), F32)
    for b in range(4):
        velocity += vel[b].astype(F32)
    zscore = (moved + step_size * velocity) / spread
    own_squares = jnp.where(live, zscore * zscore, 0.0)
    slot = z * 2 + core
    squares[slot] = jnp.sum(own_squares.reshape(ROWS // 8, 8, 128), axis=0)
    sq_index = 0
    sq_waits = []
    for dz in range(4):
        for dc in (0, 1):
            if dz == 0 and dc == 0:
                continue
            to_core_id = (core + dc) % 2
            send(squares.at[slot], squares.at[slot], R_SQ + sq_index, at(sec, x, (z + dz) % 4, yl, to_core_id))
            sq_waits.append((((z + 4 - dz) % 4) * 2 + to_core_id, R_SQ + sq_index))
            sq_index += 1

    batch = rewards_ref.shape[1]
    reward = rewards_ref[...].astype(F32)
    group = groups_ref[...].astype(F32)
    mine = iota((1, batch), 1) == x
    own_group = jnp.sum(jnp.where(mine, group, 0.0), axis=1, keepdims=True)
    own_reward = jnp.sum(jnp.where(mine, reward, 0.0), axis=1, keepdims=True)
    member = jnp.where(group == own_group, 1.0, 0.0)
    mean = jnp.sum(member * reward, axis=1, keepdims=True) / GROUP
    centered = reward - mean
    variance = jnp.sum(member * centered * centered, axis=1, keepdims=True) / GROUP
    advantage = (own_reward - mean) / (jnp.sqrt(variance) + 1.0)

    for index, recv in sq_waits:
        arrive(squares.at[index], recv)
    clip_squares = jnp.zeros((8, 128), F32)
    for b in range(8):
        clip_squares += squares[b]
    clip_squares = jnp.sum(jnp.sum(clip_squares, axis=1, keepdims=True), axis=0, keepdims=True)
    ratio = jnp.exp(-0.5 * clip_squares / count - one * rollout_ref[x])
    out_ratio[...] = jnp.broadcast_to(ratio, (8, 128))
    low_edge, high_edge = 1.0 - clip_range, 1.0 + clip_range
    inside = (ratio >= low_edge) & (ratio <= high_edge)
    active = inside | ((advantage > 0) & (ratio < low_edge)) | ((advantage < 0) & (ratio > high_edge))
    weight = jnp.where(active, -advantage * ratio / float(CLIPS), 0.0)

    grad_vel = jnp.where(live, -weight * zscore * step_size / (spread * count), 0.0).astype(BF16)
    for b in (0, 1):
        gout[b * ROWS : (b + 1) * ROWS, :] = dot_nt(grad_vel, wide[b]).astype(BF16)

    def backward(i, carry):
        head = i // 2
        cols = lanes(head * HD, HD)
        rows = rows_at((i % 2) * ROWS, ROWS)
        query, grad = queries[rows, cols], gout[rows, cols]
        shift_row = top[head, rows, :][:, 0:1]
        delta = jnp.sum(grad.astype(F32) * attn[rows, cols].astype(F32), axis=1, keepdims=True)

        def plane_step(p, grad_sum):
            plane_rows = rows_at(p * PLANE, PLANE, PLANE)
            key = keys[plane_rows, cols]
            probabilities = jnp.exp2(dot_nt(query, key) + key_bias(p * PLANE) - shift_row)
            grad_probs = dot_nt(grad, values[plane_rows, cols])
            grad_scores = (probabilities * (grad_probs - delta)).astype(BF16)
            return grad_sum + dot(grad_scores, key)

        grad_sum = lax.fori_loop(0, 4, plane_step, jnp.zeros((ROWS, HD), F32))
        gq[rows, cols] = (grad_sum * head_scale).astype(BF16)
        return carry

    lax.fori_loop(0, 6, backward, 0)

    for b in (0, 1):
        part = dot_nt(gq[b * ROWS : (b + 1) * ROWS, :], upb[:, 0:OWN]) * out_scale
        glow_send[b] = part.astype(BF16)
    for d in (1, 2, 3):
        other, device = y_peer(d)
        send(glow_send.at[other % 2], glow.at[y], R_LOW + d - 1, device)
    glow[y] = glow_send[yl]
    up_part = dot(jnp.transpose(low[...].astype(F32)).astype(BF16), gq[...])
    du[0, :, 768:1024] = up_part[:, 0:256]
    du[1, :, 768:896] = up_part[:, 256:384]
    du[1, :, 896:1024] = jnp.zeros((128, 128), F32)
    for d in (1, 2, 3):
        arrive(glow.at[(y + 4 - d) % 4], R_LOW + d - 1)
    low_sum = jnp.zeros((ROWS, 128), F32)
    for b in range(4):
        low_sum += glow[b].astype(F32)
    low_turned = jnp.transpose(low_sum).astype(BF16)

    for half in (1, 0):
        where = (core + half) % 2
        for j in range(3):
            cols = lanes(sec * HALF + where * 768 + j * 256, 256)
            du[where, :, j * 256 : (j + 1) * 256] = dot(low_turned, normed[:, cols])
        if half == 1:
            send(du.at[where], core_recv, R_RC, other_core)
    arrive(core_recv, R_RC)
    xs[...] = (du[core] + core_recv[...]).astype(BF16)
    for d in (1, 2, 3):
        to = (x + d) % 4
        send(xs.at[rows_at(to * 32, 32, 32), :], xr.at[d - 1], R_RX + d - 1, at(sec, to, z, yl, core))
    slab = du[core, x_rows, :] + core_recv[x_rows, :]
    for d in (1, 2, 3):
        arrive(xr.at[d - 1], R_RX + d - 1)
        slab += xr[d - 1].astype(F32)
    zs[...] = slab
    for d in (1, 2, 3):
        to = (z + d) % 4
        send(zs.at[rows_at(to * 8, 8, 8), :], zr.at[d - 1], R_RZ + d - 1, at(sec, x, to, yl, core))
    z_rows = rows_at(z * 8, 8, 8)
    piece = zs[z_rows, :]
    for d in (1, 2, 3):
        arrive(zr.at[d - 1], R_RZ + d - 1)
        piece += zr[d - 1]
    yr[y] = piece
    for d in (1, 2, 3):
        send(yr.at[y], yr.at[y], R_RY + d - 1, y_peer(d)[1])
    for d in (1, 2, 3):
        arrive(yr.at[(y + 4 - d) % 4], R_RY + d - 1)
    for b in (0, 1):
        zg[z_rows, b * 768 : (b + 1) * 768] = yr[2 * b, :, 0:768] + yr[2 * b + 1, :, 0:768]
        zg[z_rows, HALF + b * 256 : HALF + (b + 1) * 256] = yr[sec * 2 + b, :, 768:1024]

    for d in (1, 2, 3):
        send(zg.at[z_rows, :], zg.at[z_rows, :], R_GZ + d - 1, at(sec, x, (z + d) % 4, yl, core))
    for d in (1, 2, 3):
        arrive(zg.at[rows_at(((z + 4 - d) % 4) * 8, 8, 8), :], R_GZ + d - 1)
    full[core, x_rows, :] = zg[...].astype(BF16)
    mine_full = full.at[core, x_rows, :]
    for d in (1, 2, 3):
        send(mine_full, mine_full, R_GX + d - 1, at(sec, (x + d) % 4, z, yl, core))
    send(mine_full, mine_full, R_GC, other_core)
    for d in (1, 2, 3):
        from_rows = rows_at(((x + 4 - d) % 4) * 32, 32, 32)
        arrive(full.at[core, from_rows, :], R_GX + d - 1)
        send(full.at[core, from_rows, :], full.at[core, from_rows, :], R_GC + d, other_core)
    for d in (0, 1, 2, 3):
        from_rows = rows_at(((x + 4 - d) % 4) * 32, 32, 32)
        arrive(full.at[1 - core, from_rows, :], R_GC + d)

    norm_sum = jnp.zeros((128, 256), F32)
    for b in (0, 1):
        for j in range(HALF // 256):
            part = full[b, :, j * 256 : (j + 1) * 256].astype(F32)
            norm_sum += part * part
    norm_sum = jnp.sum(jnp.sum(norm_sum, axis=1, keepdims=True), axis=0, keepdims=True)
    factor = step_length / jnp.sqrt(norm_sum * (input_scale * input_scale) + norm_eps)
    down_factor, up_factor = factor * input_scale, factor * out_scale
    for t in range(MODEL_WIDTH // 128):
        part = full[(t % 12) // 6, :, (t // 12) * 768 + (t % 6) * 128 : (t // 12) * 768 + (t % 6) * 128 + 128]
        rows = slice(t * 128, (t + 1) * 128)
        out_down[rows, :] = down_ref[rows, :] - down_factor * jnp.transpose(part.astype(F32))
    for b in (0, 1):
        for c, width in ((0, 256), (1, 128)):
            cols = slice(b * OWN + c * 256, b * OWN + c * 256 + width)
            part = full[c, :, HALF + b * 256 : HALF + b * 256 + width].astype(F32)
            out_up[:, cols] = up_ref[:, cols] - up_factor * part

    for copy in pending:
        copy.wait_send()


def shards(
    trajectory, block_input, chosen, lengths, rewards, prompt_group_index, rollout_log_probability,
    timestep_norm_shift, patch_input_weight, frozen_query_matrix, frozen_key_matrix, frozen_value_matrix,
    velocity_output_weight, adapter_down_factor, adapter_up_factor,
):
    vmem = pl.BlockSpec(memory_space=pltpu.VMEM)
    smem = pl.BlockSpec(memory_space=pltpu.SMEM)
    hbm = pl.BlockSpec(memory_space=pl.ANY)
    V = pltpu.VMEM
    scratch = [
        V((ROWS, MODEL_WIDTH), BF16),
        V((MODEL_WIDTH, 2 * OWN), BF16),
        V((MODEL_WIDTH, 2 * OWN), BF16),
        V((MODEL_WIDTH, 2 * OWN), BF16),
        V((MODEL_WIDTH, ADAPTER_RANK), BF16),
        V((ADAPTER_RANK, 2 * OWN), BF16),
        V((ROWS, MODEL_WIDTH), F32),
        V((ROWS, MODEL_WIDTH), BF16),
        V((CLIPS, 2, PAIRS, 128), BF16),
        V((2, 2, 128, 128), BF16),
        V((ROWS, 2 * OWN), BF16),
        V((ROWS, 2 * OWN), BF16),
        V((ROWS, 2 * OWN), BF16),
        V((4 * PLANE, OWN), BF16),
        V((4 * PLANE, OWN), BF16),
        V((2 * ROWS, OWN), BF16),
        V((2 * ROWS, ADAPTER_RANK), BF16),
        V((3, 2 * ROWS, 128), F32),
        V((3, 2 * ROWS, 128), F32),
        V((2 * ROWS, OWN), F32),
        V((2 * ROWS, OWN), BF16),
        V((4, ROWS, 128), BF16),
        V((8, 8, 128), F32),
        V((2 * ROWS, OWN), BF16),
        V((2 * ROWS, OWN), BF16),
        V((2, ROWS, 128), BF16),
        V((4, ROWS, 128), BF16),
        V((2, 128, 1024), F32),
        V((128, 1024), F32),
        V((128, 1024), BF16),
        V((3, 32, 1024), BF16),
        V((32, 1024), F32),
        V((3, 8, 1024), F32),
        V((4, 8, 1024), F32),
        V((32, 2048), F32),
        V((2, 128, 2048), BF16),
        pltpu.SemaphoreType.DMA((N_SEND,)),
        pltpu.SemaphoreType.DMA((N_RECV,)),
        pltpu.SemaphoreType.DMA((8,)),
    ]
    revised_down, revised_up, ratio = pl.pallas_call(
        body,
        out_shape=(
            jax.ShapeDtypeStruct((MODEL_WIDTH, ADAPTER_RANK), F32),
            jax.ShapeDtypeStruct((ADAPTER_RANK, 2 * OWN), F32),
            jax.ShapeDtypeStruct((8, 128), F32),
        ),
        in_specs=[smem] * 3 + [vmem] * 8 + [hbm] * 4,
        out_specs=(vmem, vmem, vmem),
        scratch_shapes=scratch,
        compiler_params=pltpu.CompilerParams(
            collective_id=0, has_side_effects=True, vmem_limit_bytes=60 * 1024 * 1024
        ),
        cost_estimate=pl.CostEstimate(flops=12_000_000_000, bytes_accessed=24_000_000, transcendentals=13_000_000),
        name="policy_step",
    )(
        chosen, lengths, rollout_log_probability,
        trajectory.reshape(STEPS + 1, CLIPS, PAIRS, 128),
        rewards.reshape(1, -1), prompt_group_index.reshape(1, -1), timestep_norm_shift, patch_input_weight,
        velocity_output_weight, adapter_down_factor, adapter_up_factor,
        block_input.reshape(ROWS, MODEL_WIDTH), frozen_query_matrix, frozen_key_matrix, frozen_value_matrix,
    )
    return revised_down, revised_up, ratio[0, :1]


def solution(mesh):
    return jax.shard_map(
        shards,
        mesh=mesh,
        in_specs=(
            P(None, None, "seq", "dp", None),
            P("dp", "seq", None),
            P(), P(), P(), P(), P(), P(), P(),
            P(None, "section"),
            P(None, "section"),
            P(None, "section"),
            P("section", None),
            P(),
            P(None, "section"),
        ),
        out_specs=(P(), P(None, "section"), P("dp")),
        check_vma=False,
    )
```

time: 803 us -> 122 us (0.15)
  waiting for transfers between devices: 594 us -> 0 us
  Pallas kernels: 0 us -> 115 us
  matrix products: 73.6 us -> 0 us
  blocking collectives: 40.1 us -> 0 us
  other arithmetic: 30.8 us -> 0 us
  local copies, waits for them, and re-layouts: 30.4 us -> 6.34 us
  between operations: 20.4 us -> 0.64 us
  starting transfers between devices: 9.16 us -> 0 us
    psum x2 -> x0, waiting for transfers between devices: 569 us -> none  [the longest x1 545 us: shards(): down_gradient = lax.psum(down_term, ('dp', 'seq'))]
    pallas_call x0 -> x1, Pallas kernels: none -> 115 us  [shards(): pl.pallas_call(body, out_shape=(jax.ShapeDtypeStruct((MODEL_WIDTH, ADAPTE...]
    dot_general x14 -> x0, matrix products: 73.6 us -> none  [the longest x1 18.4 us: return_block(): jnp.einsum('chqk,ckhd->cqhd', grad_scores, key_heads, preferred_element_t...]
    psum x2 -> x0, blocking collectives: 40.1 us -> none  [the longest x1 29.6 us: shards(): clip_squares = lax.psum(jnp.sum(squares, axis=(1, 2)), 'seq')]
    all_gather x2 -> x0, waiting for transfers between devices: 23.7 us -> none  [the longest x1 16.3 us: shards(): lax.all_gather(key_proj, 'seq', axis=1, tiled=True)]
    reduce_sum x10 -> x0, other arithmetic: 21.8 us -> none  [the longest x1 12.9 us: attend_block(): totals = jnp.sum(exp_scores, axis=3)]
    all_gather x2 -> x0, local copies, waits for them, and re-layouts: 17.3 us -> none  [the longest x1 8.74 us: shards(): lax.all_gather(key_proj, 'seq', axis=1, tiled=True)]
    all_to_all x2 -> x0, starting transfers between devices: 8.85 us -> none  [the longest x1 4.84 us: shards(): lax.all_to_all(current_all, 'dp', split_axis=0, concat_axis=2, tiled=True)]
  transfers between devices with their start and end apart: 6 -> 0, of which waited for: 5 -> 0; matrix products, arithmetic and copies ran while one was open for 8% -> 0% of each run, Pallas kernels for 0% -> 0%
where the time goes in v1:
time: 122 us
  Pallas kernels  115 us (94%)
  local copies, waits for them, and re-layouts  6.34 us (5%)
    pallas_call x1, Pallas kernels, shards(): pl.pallas_call(body, out_shape=(jax.ShapeDtypeStruct((MODEL_WIDTH, ADAPTE...  115 us
    unnamed x5, local copies, waits for them, and re-layouts  5.16 us

profile of v1, /device:TPU:1, one launch (start us, length us, event | category | flops | bytes accessed | tf_op | source)
XLA Modules:
  0.0 122.2 jit_solution(3504799547404256242)
XLA Ops:
  0.6 1.7 %copy.18.wout_ref = bf16[768,64]{1,0:T(8,128)(2,1)} copy(bf16[768,64]{0,1:T(8,128)(2,1)} %param.27) | data formatting | bytes 196608 | tf_op args[12]
  2.3 115.2 %policy_step.1 = (f32[3072,128]{1,0:T(8,128)}, f32[128,768]{1,0:T(8,128)}, f32[8,128]{1,0:T(8,128)}) custom-call(s32[4]{0:T(128)} %chosen_ref.1, s32[4]{0:T(128)} %lengths_ref.1, f32[4]{0:T(128)} %rollout_ref.1, bf16[5,4,32,128]{3,2,1,0:T(8,128)(2,1)} %bitcast.6, s32[1,64]{1,0:T(1,128)} %bitcast.7, s32[1,64]{1,0:T(1,128)} %bitcast.8, ...), custom_call_target="tpu_custom_call" | custom-call | flops 12000000000 | bytes 24000000 | tf_op jit(solution)/shard_map/policy_step/pallas_call | solution.py:572
  117.6 1.2 slice.3
  118.7 0.0 copy-start
  118.7 2.7 %copy.21 = f32[3072,128]{1,0:T(8,128)} copy(f32[3072,128]{1,0:T(8,128)} %get-tuple-element.12) | data formatting | bytes 3145728
  121.4 0.0 copy-done
  121.4 0.7 copy.22
Async XLA Ops:
  118.7 2.7 %copy-start = (f32[128,768]{1,0:T(8,128)S(1)}, f32[128,768]{1,0:T(8,128)}, u32[]{:S(2)}) copy-start(f32[128,768]{1,0:T(8,128)} %get-tuple-element.13) | copy-start | bytes 1179652

commit v2 on v1

--- a/solution.py
+++ b/solution.py
@@ -79,10 +79,10 @@
 
 def body(
     chosen_ref, lengths_ref, rollout_ref,
-    traj_ref, rewards_ref, groups_ref, shift_ref, patch_ref, wout_ref, down_ref, up_ref,
-    x_hbm, wq_hbm, wk_hbm, wv_hbm,
-    out_down, out_up, out_ratio,
-    xin, wq, wk, wv, downb, upb, emb, normed,
+    traj_ref, rewards_ref, groups_ref,
+    shift_hbm, patch_hbm, wout_hbm, down_hbm, up_hbm, x_hbm, wq_hbm, wk_hbm, wv_hbm,
+    out_grad, out_ratio,
+    shift_ref, patch_ref, wout_ref, down_ref, up_ref, xin, wq, wk, wv, downb, upb, emb, normed,
     sel, latents, stage_k, stage_v, stage_q, keys, values, queries, low,
     top, total, acc, attn, vel, squares, gout, gq, glow_send, glow,
     du, core_recv, xs, xr, zs, zr, yr, zg, full,
@@ -132,11 +132,6 @@
         loads.append(copy)
         return copy
 
-    load_x = load(x_hbm, xin)
-    own_cols, other_cols = lanes(yl * OWN, OWN), lanes((1 - yl) * OWN, OWN)
-    load_w = []
-    for src, dst in ((wk_hbm, wk), (wv_hbm, wv), (wq_hbm, wq)):
-        load_w.append((load(src.at[:, own_cols], dst.at[:, 0:OWN]), load(src.at[:, other_cols], dst.at[:, OWN : 2 * OWN])))
 
     peers = [at(sec, (x + d) % 4, z, yl, core) for d in (1, 2, 3)]
     peers += [y_peer(d)[1] for d in (1, 2, 3)]
@@ -146,6 +141,13 @@
     for peer in peers:
         pl.semaphore_signal(barrier, inc=1, device_id=peer, device_id_type=MESH)
 
+    load_x = [load(x_hbm, xin), load(patch_hbm, patch_ref), load(shift_hbm, shift_ref)]
+    own_cols, other_cols = lanes(yl * OWN, OWN), lanes((1 - yl) * OWN, OWN)
+    load_w = []
+    for src, dst in ((wk_hbm, wk), (wv_hbm, wv), (wq_hbm, wq)):
+        load_w.append((load(src.at[:, own_cols], dst.at[:, 0:OWN]), load(src.at[:, other_cols], dst.at[:, OWN : 2 * OWN])))
+    load_adapter = [load(down_hbm, down_ref), load(up_hbm, up_ref), load(wout_hbm.at[:, own_cols], wout_ref)]
+
     for c in range(CLIPS):
         sel[c, 0] = traj_ref[chosen_ref[c], c]
         sel[c, 1] = traj_ref[chosen_ref[c] + 1, c]
@@ -156,10 +158,6 @@
         send(sel.at[to], latents.at[yl, :, x_rows, :], R_X + d - 1, at(sec, to, z, yl, core))
     latents[yl, :, x_rows, :] = sel[x]
 
-    downb[...] = down_ref[...].astype(BF16)
-    upb[:, 0:OWN] = up_ref[:, own_cols].astype(BF16)
-    upb[:, OWN : 2 * OWN] = up_ref[:, other_cols].astype(BF16)
-
     chosen = chosen_ref[x]
     length = lengths_ref[x]
     one = jnp.ones((1, 1), F32)
@@ -182,7 +180,8 @@
     send(latents.at[yl], latents.at[yl], R_PAIR + 4, partner)
 
     now_tokens = dot(token_rows(latents[yl, 0]), fold(0, 64)).astype(BF16)
-    load_x.wait()
+    for copy in load_x:
+        copy.wait()
     squares_sum = jnp.zeros((ROWS, 1), F32)
     chunk = 512
     for j in range(MODEL_WIDTH // chunk):
@@ -265,6 +264,11 @@
         to_core(0, 0, kv)
     own_rows = rows_at(yl * ROWS, ROWS)
     pair_rows = rows_at((1 - yl) * ROWS, ROWS)
+    for copy in load_adapter:
+        copy.wait()
+    downb[...] = down_ref[...].astype(BF16)
+    upb[:, 0:OWN] = up_ref[:, own_cols].astype(BF16)
+    upb[:, OWN : 2 * OWN] = up_ref[:, other_cols].astype(BF16)
     low_own = (dot(normed[...], downb[...]) * input_scale).astype(BF16)
     low[own_rows, :] = low_own
     project(wq, load_w[2], stage_q, low_own, query_scale)
@@ -279,34 +283,49 @@
     def key_bias(start):
         return jnp.where(start + iota((1, PLANE), 1) < length, 0.0, masked_score)
 
+    def repeat(stat, count):
+        return jnp.concatenate([stat] * count, axis=1)
+
+    def fold_lanes(op, tile):
+        out = tile[:, 0:128]
+        for j in range(1, tile.shape[1] // 128):
+            out = op(out, tile[:, j * 128 : (j + 1) * 128])
+        return out
+
     def forward_plane(plane):
         start = ((z + plane) % 4) * PLANE
         plane_rows = rows_at(start, PLANE, PLANE)
         bias = key_bias(start)
         first = plane == 0
-
-        def step(i, carry):
-            head = i // 2
-            cols = lanes(head * HD, HD)
-            rows = rows_at((i % 2) * ROWS, ROWS)
-            scores = dot_nt(queries[rows, cols], keys[plane_rows, cols]) + bias
-            peak = jnp.max(scores, axis=1, keepdims=True)
+        tiles = [(h, slice(h * HD, (h + 1) * HD), slice(b * ROWS, (b + 1) * ROWS)) for h in range(3) for b in (0, 1)]
+
+        def score(tile):
+            _, cols, rows = tile
+            return dot_nt(queries[rows, cols], keys[plane_rows, cols]) + bias
+
+        def softmax(tile, scores):
+            head, cols, rows = tile
+            peak = jnp.max(fold_lanes(jnp.maximum, scores), axis=1, keepdims=True)
+            peak = jnp.broadcast_to(peak, (ROWS, 128))
             if not first:
-                before = top[head, rows, :][:, 0:1]
+                before = top[head, rows, :]
                 peak = jnp.maximum(peak, before)
-            exp_scores = jnp.exp2(scores - peak)
-            sums = jnp.sum(exp_scores, axis=1, keepdims=True)
+            exp_scores = jnp.exp2(scores - repeat(peak, PLANE // 128))
+            sums = fold_lanes(jnp.add, exp_scores)
             weighted = dot(exp_scores.astype(BF16), values[plane_rows, cols])
             if not first:
                 decay = jnp.exp2(before - peak)
-                sums += decay * total[head, rows, :][:, 0:1]
+                sums += decay * total[head, rows, :]
                 weighted += decay * acc[rows, cols]
-            top[head, rows, :] = jnp.broadcast_to(peak, (ROWS, 128))
-            total[head, rows, :] = jnp.broadcast_to(sums, (ROWS, 128))
+            top[head, rows, :] = peak
+            total[head, rows, :] = sums
             acc[rows, cols] = weighted
-            return carry
-
-        lax.fori_loop(0, 6, step, 0)
+
+        scores = score(tiles[0])
+        for i, tile in enumerate(tiles):
+            ahead = score(tiles[i + 1]) if i + 1 < len(tiles) else None
+            softmax(tile, scores)
+            scores = ahead
 
     for kv in (0, 1):
         for above in (0, 1):
@@ -332,19 +351,16 @@
         head = i // 2
         cols = lanes(head * HD, HD)
         rows = rows_at((i % 2) * ROWS, ROWS)
-        sums = total[head, rows, :]
+        sums = jnp.broadcast_to(jnp.sum(total[head, rows, :], axis=1, keepdims=True), (ROWS, 128))
         attn[rows, cols] = (acc[rows, cols] / sums).astype(BF16)
         top[head, rows, :] = top[head, rows, :] + jnp.log(sums) * math.log2(math.e)
         return carry
 
     lax.fori_loop(0, 6, finish_head, 0)
 
-    wout = wout_ref[rows_at(yl * OWN, OWN, 128), :]
-    spread_cols = [
-        jnp.where(iota((PATCH, 128), 0) + PATCH * b == iota((PATCH, 128), 1), 1.0, 0.0).astype(BF16) for b in (0, 1)
-    ]
-    wide = [dot(wout, cols).astype(BF16) for cols in spread_cols]
-    partial = dot(attn[0:ROWS, :], wide[0]) + dot(attn[ROWS : 2 * ROWS, :], wide[1])
+    blank = jnp.zeros((PATCH, OWN), BF16)
+    wide = [jnp.concatenate([wout_ref[...], blank], axis=0), jnp.concatenate([blank, wout_ref[...]], axis=0)]
+    partial = dot_nt(attn[0:ROWS, :], wide[0]) + dot_nt(attn[ROWS : 2 * ROWS, :], wide[1])
     vel[y] = partial.astype(BF16)
     for d in (1, 2, 3):
         send(vel.at[y], vel.at[y], R_VEL + d - 1, y_peer(d)[1])
@@ -377,6 +393,40 @@
             sq_waits.append((((z + 4 - dz) % 4) * 2 + to_core_id, R_SQ + sq_index))
             sq_index += 1
 
+    grad_vel = jnp.where(live, -zscore * step_size / (spread * count), 0.0).astype(BF16)
+    for b in (0, 1):
+        gout[b * ROWS : (b + 1) * ROWS, :] = dot(grad_vel, wide[b]).astype(BF16)
+
+    for head in range(3):
+        cols = slice(head * HD, (head + 1) * HD)
+        delta = jnp.sum(gout[:, cols].astype(F32) * attn[:, cols].astype(F32), axis=1, keepdims=True)
+        total[head] = jnp.broadcast_to(delta, (2 * ROWS, 128))
+    acc[...] = jnp.zeros_like(acc)
+
+    def backward_plane(p, carry):
+        plane_rows = rows_at(p * PLANE, PLANE, PLANE)
+        bias = key_bias(p * PLANE)
+
+        def products(head):
+            cols = slice(head * HD, (head + 1) * HD)
+            scores = dot_nt(queries[:, cols], keys[plane_rows, cols]) + bias
+            return scores, dot_nt(gout[:, cols], values[plane_rows, cols])
+
+        def gradient(head, scores, grad_probs):
+            cols = slice(head * HD, (head + 1) * HD)
+            probabilities = jnp.exp2(scores - repeat(top[head], PLANE // 128))
+            grad_scores = (probabilities * (grad_probs - repeat(total[head], PLANE // 128))).astype(BF16)
+            acc[:, cols] += dot(grad_scores, keys[plane_rows, cols])
+
+        made = products(0)
+        for head in range(3):
+            ahead = products(head + 1) if head < 2 else None
+            gradient(head, *made)
+            made = ahead
+        return carry
+
+    lax.fori_loop(0, 4, backward_plane, 0)
+
     batch = rewards_ref.shape[1]
     reward = rewards_ref[...].astype(F32)
     group = groups_ref[...].astype(F32)
@@ -402,31 +452,7 @@
     active = inside | ((advantage > 0) & (ratio < low_edge)) | ((advantage < 0) & (ratio > high_edge))
     weight = jnp.where(active, -advantage * ratio / float(CLIPS), 0.0)
 
-    grad_vel = jnp.where(live, -weight * zscore * step_size / (spread * count), 0.0).astype(BF16)
-    for b in (0, 1):
-        gout[b * ROWS : (b + 1) * ROWS, :] = dot_nt(grad_vel, wide[b]).astype(BF16)
-
-    def backward(i, carry):
-        head = i // 2
-        cols = lanes(head * HD, HD)
-        rows = rows_at((i % 2) * ROWS, ROWS)
-        query, grad = queries[rows, cols], gout[rows, cols]
-        shift_row = top[head, rows, :][:, 0:1]
-        delta = jnp.sum(grad.astype(F32) * attn[rows, cols].astype(F32), axis=1, keepdims=True)
-
-        def plane_step(p, grad_sum):
-            plane_rows = rows_at(p * PLANE, PLANE, PLANE)
-            key = keys[plane_rows, cols]
-            probabilities = jnp.exp2(dot_nt(query, key) + key_bias(p * PLANE) - shift_row)
-            grad_probs = dot_nt(grad, values[plane_rows, cols])
-            grad_scores = (probabilities * (grad_probs - delta)).astype(BF16)
-            return grad_sum + dot(grad_scores, key)
-
-        grad_sum = lax.fori_loop(0, 4, plane_step, jnp.zeros((ROWS, HD), F32))
-        gq[rows, cols] = (grad_sum * head_scale).astype(BF16)
-        return carry
-
-    lax.fori_loop(0, 6, backward, 0)
+    gq[...] = (acc[...] * (head_scale * weight)).astype(BF16)
 
     for b in (0, 1):
         part = dot_nt(gq[b * ROWS : (b + 1) * ROWS, :], upb[:, 0:OWN]) * out_scale
@@ -497,26 +523,30 @@
         from_rows = rows_at(((x + 4 - d) % 4) * 32, 32, 32)
         arrive(full.at[1 - core, from_rows, :], R_GC + d)
 
+    out_grad[...] = full[...]
+    for copy in pending:
+        copy.wait_send()
+
+
+def update(grad_ref, down_ref, up_ref, ratio_ref, out_down, out_up, out_ratio):
     norm_sum = jnp.zeros((128, 256), F32)
     for b in (0, 1):
         for j in range(HALF // 256):
-            part = full[b, :, j * 256 : (j + 1) * 256].astype(F32)
+            part = grad_ref[b, :, j * 256 : (j + 1) * 256].astype(F32)
             norm_sum += part * part
     norm_sum = jnp.sum(jnp.sum(norm_sum, axis=1, keepdims=True), axis=0, keepdims=True)
     factor = step_length / jnp.sqrt(norm_sum * (input_scale * input_scale) + norm_eps)
     down_factor, up_factor = factor * input_scale, factor * out_scale
     for t in range(MODEL_WIDTH // 128):
-        part = full[(t % 12) // 6, :, (t // 12) * 768 + (t % 6) * 128 : (t // 12) * 768 + (t % 6) * 128 + 128]
+        part = grad_ref[(t % 12) // 6, :, (t // 12) * 768 + (t % 6) * 128 : (t // 12) * 768 + (t % 6) * 128 + 128]
         rows = slice(t * 128, (t + 1) * 128)
         out_down[rows, :] = down_ref[rows, :] - down_factor * jnp.transpose(part.astype(F32))
     for b in (0, 1):
         for c, width in ((0, 256), (1, 128)):
             cols = slice(b * OWN + c * 256, b * OWN + c * 256 + width)
-            part = full[c, :, HALF + b * 256 : HALF + b * 256 + width].astype(F32)
+            part = grad_ref[c, :, HALF + b * 256 : HALF + b * 256 + width].astype(F32)
             out_up[:, cols] = up_ref[:, cols] - up_factor * part
-
-    for copy in pending:
-        copy.wait_send()
+    out_ratio[0] = jnp.sum(ratio_ref[0:1, 0:1])
 
 
 def shards(
@@ -529,6 +559,11 @@
     hbm = pl.BlockSpec(memory_space=pl.ANY)
     V = pltpu.VMEM
     scratch = [
+        V((STEPS, 2, MODEL_WIDTH), F32),
+        V((PATCH, MODEL_WIDTH), BF16),
+        V((PATCH, OWN), BF16),
+        V((MODEL_WIDTH, ADAPTER_RANK), F32),
+        V((ADAPTER_RANK, 2 * OWN), F32),
         V((ROWS, MODEL_WIDTH), BF16),
         V((MODEL_WIDTH, 2 * OWN), BF16),
         V((MODEL_WIDTH, 2 * OWN), BF16),
@@ -567,17 +602,16 @@
         V((2, 128, 2048), BF16),
         pltpu.SemaphoreType.DMA((N_SEND,)),
         pltpu.SemaphoreType.DMA((N_RECV,)),
-        pltpu.SemaphoreType.DMA((8,)),
+        pltpu.SemaphoreType.DMA((16,)),
     ]
-    revised_down, revised_up, ratio = pl.pallas_call(
+    gradients, ratio = pl.pallas_call(
         body,
         out_shape=(
-            jax.ShapeDtypeStruct((MODEL_WIDTH, ADAPTER_RANK), F32),
-            jax.ShapeDtypeStruct((ADAPTER_RANK, 2 * OWN), F32),
+            jax.ShapeDtypeStruct((2, ADAPTER_RANK, 2048), BF16),
             jax.ShapeDtypeStruct((8, 128), F32),
         ),
-        in_specs=[smem] * 3 + [vmem] * 8 + [hbm] * 4,
-        out_specs=(vmem, vmem, vmem),
+        in_specs=[smem] * 3 + [vmem] * 3 + [hbm] * 9,
+        out_specs=(vmem, vmem),
         scratch_shapes=scratch,
         compiler_params=pltpu.CompilerParams(
             collective_id=0, has_side_effects=True, vmem_limit_bytes=60 * 1024 * 1024
@@ -588,10 +622,21 @@
         chosen, lengths, rollout_log_probability,
         trajectory.reshape(STEPS + 1, CLIPS, PAIRS, 128),
         rewards.reshape(1, -1), prompt_group_index.reshape(1, -1), timestep_norm_shift, patch_input_weight,
-        velocity_output_weight, adapter_down_factor, adapter_up_factor,
+        velocity_output_weight.T, adapter_down_factor, adapter_up_factor,
         block_input.reshape(ROWS, MODEL_WIDTH), frozen_query_matrix, frozen_key_matrix, frozen_value_matrix,
     )
-    return revised_down, revised_up, ratio[0, :1]
+    return pl.pallas_call(
+        update,
+        out_shape=(
+            jax.ShapeDtypeStruct((MODEL_WIDTH, ADAPTER_RANK), F32),
+            jax.ShapeDtypeStruct((ADAPTER_RANK, 2 * OWN), F32),
+            jax.ShapeDtypeStruct((1,), F32),
+        ),
+        in_specs=[vmem] * 4,
+        out_specs=(vmem, vmem, smem),
+        compiler_params=pltpu.CompilerParams(vmem_limit_bytes=32 * 1024 * 1024),
+        name="update",
+    )(gradients, adapter_down_factor, adapter_up_factor, ratio)
 
 
 def solution(mesh):

time: 122 us -> 104 us (0.85)
  Pallas kernels: 115 us -> 101 us
  local copies, waits for them, and re-layouts: 6.34 us -> 1.91 us
    pallas_call x1 -> x2, Pallas kernels: 115 us -> 101 us  [the longest x1 99.6 us: shards(): pl.pallas_call(body, out_shape=(jax.ShapeDtypeStruct((2, ADAPTER_RANK, 20...]
    unnamed x5 -> x8, local copies, waits for them, and re-layouts: 5.16 us -> 1.91 us
where the time goes in v2:
time: 104 us
  Pallas kernels  101 us (97%)
  local copies, waits for them, and re-layouts  1.91 us (2%)
    pallas_call x1, Pallas kernels, shards(): pl.pallas_call(body, out_shape=(jax.ShapeDtypeStruct((2, ADAPTER_RANK, 20...  99.6 us

profile of v2, /device:TPU:1, one launch (start us, length us, event | category | flops | bytes accessed | tf_op | source)
XLA Modules:
  0.0 104.1 jit_solution(4027413884645997532)
XLA Ops:
  0.6 0.0 copy-start
  0.6 0.0 copy-start.2
  0.7 99.6 %policy_step.1 = (bf16[2,128,2048]{2,1,0:T(8,128)(2,1)}, f32[8,128]{1,0:T(8,128)}) custom-call(s32[4]{0:T(128)} %chosen_ref.1, s32[4]{0:T(128)} %lengths_ref.1, f32[4]{0:T(128)} %rollout_ref.1, bf16[5,4,32,128]{3,2,1,0:T(8,128)(2,1)} %bitcast.6, s32[1,64]{1,0:T(1,128)} %bitcast.8, s32[1,64]{1,0:T(1,128)} %bitcast.9, f32[4,2,3072]{2,1,0:T(2,128)} %shift_hbm.1, ...), custom_call_target="tpu_custom_call" | custom-call | flops 12000000000 | bytes 24000000 | tf_op jit(solution)/shard_map/policy_step/pallas_call | solution.py:607
  100.2 0.0 copy-done
  100.3 0.0 copy-done.2
  100.3 0.0 copy-start.1
  100.3 1.2 %copy-done.1 = bf16[2,128,2048]{2,1,0:T(8,128)(2,1)S(1)} copy-done((bf16[2,128,2048]{2,1,0:T(8,128)(2,1)S(1)}, bf16[2,128,2048]{2,1,0:T(8,128)(2,1)}, u32[]{:S(2)}) %copy-start.1) | copy-done | bytes 1048600
  101.5 0.0 copy-start.3
  101.5 0.7 copy-done.3
  102.2 1.7 %update.1 = (f32[3072,128]{1,0:T(8,128)}, f32[128,768]{1,0:T(8,128)}, f32[1]{0:T(128)}) custom-call(bf16[2,128,2048]{2,1,0:T(8,128)(2,1)S(1)} %copy-done.1, f32[3072,128]{1,0:T(8,128)S(1)} %copy-done, f32[128,768]{1,0:T(8,128)S(1)} %copy-done.2, f32[8,128]{1,0:T(8,128)S(1)} %copy-done.3), custom_call_target="tpu_custom_call" | custom-call | tf_op jit(solution)/shard_map/update/pallas_call | solution.py:628
Async XLA Ops:
  0.6 99.6 %copy-start = (f32[3072,128]{1,0:T(8,128)S(1)}, f32[3072,128]{1,0:T(8,128)}, u32[]{:S(2)}) copy-start(f32[3072,128]{1,0:T(8,128)} %down_ref.1) | copy-start | bytes 4718596
  0.6 99.6 %copy-start.2 = (f32[128,768]{1,0:T(8,128)S(1)}, f32[128,768]{1,0:T(8,128)}, u32[]{:S(2)}) copy-start(f32[128,768]{1,0:T(8,128)} %up_ref.1) | copy-start | bytes 1179652
  100.3 1.2 %copy-start.1 = (bf16[2,128,2048]{2,1,0:T(8,128)(2,1)S(1)}, bf16[2,128,2048]{2,1,0:T(8,128)(2,1)}, u32[]{:S(2)}) copy-start(bf16[2,128,2048]{2,1,0:T(8,128)(2,1)} %get-tuple-element.5.grad_ref) | copy-start | bytes 3145732
  101.5 0.7 copy-start.3

commit v3 on v2

--- a/solution.py
+++ b/solution.py
@@ -45,16 +45,18 @@
 R_CORE = 20
 R_VEL = 36
 R_SQ = 39
-R_LOW = 46
-R_RC = 49
-R_RX = 50
-R_RZ = 53
-R_RY = 56
-R_GZ = 59
-R_GX = 62
-R_GC = 65
-N_RECV = 69
-N_SEND = 96
+R_LOW = 43
+R_RC = 46
+R_RS = 47
+R_RY = 62
+R_AG = 65
+R_GC = 80
+N_RECV = 96
+N_SEND = 112
+AROUND = sorted(
+    ((dx, dz) for dx in range(4) for dz in range(4) if dx or dz),
+    key=lambda d: min(d[0], 4 - d[0]) + min(d[1], 4 - d[1]),
+)
 
 
 def dot(a, b):
@@ -82,10 +84,10 @@
     traj_ref, rewards_ref, groups_ref,
     shift_hbm, patch_hbm, wout_hbm, down_hbm, up_hbm, x_hbm, wq_hbm, wk_hbm, wv_hbm,
     out_grad, out_ratio,
-    shift_ref, patch_ref, wout_ref, down_ref, up_ref, xin, wq, wk, wv, downb, upb, emb, normed,
+    shift_ref, patch_ref, wout_ref, down_ref, up_ref, xin, wk, wv, downb, upb, emb, normed,
     sel, latents, stage_k, stage_v, stage_q, keys, values, queries, low,
-    top, total, acc, attn, vel, squares, gout, gq, glow_send, glow,
-    du, core_recv, xs, xr, zs, zr, yr, zg, full,
+    top, peaks, probs, total, acc, attn, vel, squares, both, gout, gq, glow_send, glow,
+    du, core_recv, xs, xr, yr, full,
     send_sem, recv_sem, local_sem,
 ):
     sec = lax.axis_index("section")
@@ -133,19 +135,20 @@
         return copy
 
 
-    peers = [at(sec, (x + d) % 4, z, yl, core) for d in (1, 2, 3)]
+    peers = [at(sec, (x + dx) % 4, (z + dz) % 4, yl, core) for dx, dz in AROUND]
     peers += [y_peer(d)[1] for d in (1, 2, 3)]
-    peers += [at(sec, x, (z + d) % 4, yl, core) for d in (1, 2, 3)]
-    peers += [at(sec, x, (z + d) % 4, yl, 1 - core) for d in (0, 1, 2, 3)]
+    peers += [other_core]
     barrier = pltpu.get_barrier_semaphore()
     for peer in peers:
         pl.semaphore_signal(barrier, inc=1, device_id=peer, device_id_type=MESH)
 
     load_x = [load(x_hbm, xin), load(patch_hbm, patch_ref), load(shift_hbm, shift_ref)]
     own_cols, other_cols = lanes(yl * OWN, OWN), lanes((1 - yl) * OWN, OWN)
-    load_w = []
-    for src, dst in ((wk_hbm, wk), (wv_hbm, wv), (wq_hbm, wq)):
-        load_w.append((load(src.at[:, own_cols], dst.at[:, 0:OWN]), load(src.at[:, other_cols], dst.at[:, OWN : 2 * OWN])))
+
+    def load_weight(src, dst):
+        return load(src.at[:, own_cols], dst.at[:, 0:OWN]), load(src.at[:, other_cols], dst.at[:, OWN : 2 * OWN])
+
+    load_w = [load_weight(wk_hbm, wk), load_weight(wv_hbm, wv)]
     load_adapter = [load(down_hbm, down_ref), load(up_hbm, up_ref), load(wout_hbm.at[:, own_cols], wout_ref)]
 
     for c in range(CLIPS):
@@ -262,6 +265,8 @@
         store[kv][own_block, :] = stage[:, 0:OWN]
         to_z(0, kv)
         to_core(0, 0, kv)
+        if kv == 0:
+            load_w.append(load_weight(wq_hbm, wk))
     own_rows = rows_at(yl * ROWS, ROWS)
     pair_rows = rows_at((1 - yl) * ROWS, ROWS)
     for copy in load_adapter:
@@ -271,7 +276,7 @@
     upb[:, OWN : 2 * OWN] = up_ref[:, other_cols].astype(BF16)
     low_own = (dot(normed[...], downb[...]) * input_scale).astype(BF16)
     low[own_rows, :] = low_own
-    project(wq, load_w[2], stage_q, low_own, query_scale)
+    project(wk, load_w[2], stage_q, low_own, query_scale)
     send(stage_q.at[:, OWN : 2 * OWN], queries.at[own_rows, :], R_PAIR + 2, partner)
     queries[own_rows, :] = stage_q[:, 0:OWN]
     send(low.at[own_rows, :], low.at[own_rows, :], R_PAIR + 3, partner)
@@ -312,12 +317,15 @@
                 peak = jnp.maximum(peak, before)
             exp_scores = jnp.exp2(scores - repeat(peak, PLANE // 128))
             sums = fold_lanes(jnp.add, exp_scores)
-            weighted = dot(exp_scores.astype(BF16), values[plane_rows, cols])
+            kept = exp_scores.astype(BF16)
+            probs[plane, head, rows, :] = kept
+            weighted = dot(kept, values[plane_rows, cols])
             if not first:
                 decay = jnp.exp2(before - peak)
                 sums += decay * total[head, rows, :]
                 weighted += decay * acc[rows, cols]
             top[head, rows, :] = peak
+            peaks[plane, head, rows, :] = peak
             total[head, rows, :] = sums
             acc[rows, cols] = weighted
 
@@ -380,18 +388,9 @@
         velocity += vel[b].astype(F32)
     zscore = (moved + step_size * velocity) / spread
     own_squares = jnp.where(live, zscore * zscore, 0.0)
-    slot = z * 2 + core
-    squares[slot] = jnp.sum(own_squares.reshape(ROWS // 8, 8, 128), axis=0)
-    sq_index = 0
-    sq_waits = []
-    for dz in range(4):
-        for dc in (0, 1):
-            if dz == 0 and dc == 0:
-                continue
-            to_core_id = (core + dc) % 2
-            send(squares.at[slot], squares.at[slot], R_SQ + sq_index, at(sec, x, (z + dz) % 4, yl, to_core_id))
-            sq_waits.append((((z + 4 - dz) % 4) * 2 + to_core_id, R_SQ + sq_index))
-            sq_index += 1
+    squares[z] = jnp.sum(own_squares.reshape(ROWS // 8, 8, 128), axis=0)
+    for d in (1, 2, 3):
+        send(squares.at[z], squares.at[z], R_SQ + d - 1, at(sec, x, (z + d) % 4, yl, core))
 
     grad_vel = jnp.where(live, -zscore * step_size / (spread * count), 0.0).astype(BF16)
     for b in (0, 1):
@@ -403,29 +402,36 @@
         total[head] = jnp.broadcast_to(delta, (2 * ROWS, 128))
     acc[...] = jnp.zeros_like(acc)
 
-    def backward_plane(p, carry):
-        plane_rows = rows_at(p * PLANE, PLANE, PLANE)
-        bias = key_bias(p * PLANE)
-
-        def products(head):
+    def backward_plane(plane, carry):
+        plane_rows = rows_at(((z + plane) % 4) * PLANE, PLANE, PLANE)
+
+        def product(head):
             cols = slice(head * HD, (head + 1) * HD)
-            scores = dot_nt(queries[:, cols], keys[plane_rows, cols]) + bias
-            return scores, dot_nt(gout[:, cols], values[plane_rows, cols])
-
-        def gradient(head, scores, grad_probs):
+            return dot_nt(gout[:, cols], values[plane_rows, cols])
+
+        def gradient(head, grad_probs):
             cols = slice(head * HD, (head + 1) * HD)
-            probabilities = jnp.exp2(scores - repeat(top[head], PLANE // 128))
-            grad_scores = (probabilities * (grad_probs - repeat(total[head], PLANE // 128))).astype(BF16)
+            scale = jnp.exp2(peaks[plane, head] - top[head])
+            grad_scores = (grad_probs - repeat(total[head], PLANE // 128)) * repeat(scale, PLANE // 128)
+            grad_scores = (probs[plane, head].astype(F32) * grad_scores).astype(BF16)
             acc[:, cols] += dot(grad_scores, keys[plane_rows, cols])
 
-        made = products(0)
+        made = product(0)
         for head in range(3):
-            ahead = products(head + 1) if head < 2 else None
-            gradient(head, *made)
+            ahead = product(head + 1) if head < 2 else None
+            gradient(head, made)
             made = ahead
         return carry
 
-    lax.fori_loop(0, 4, backward_plane, 0)
+    lax.fori_loop(0, 2, backward_plane, 0)
+    for d in (1, 2, 3):
+        arrive(squares.at[(z + 4 - d) % 4], R_SQ + d - 1)
+    plane_squares = jnp.zeros((8, 128), F32)
+    for b in range(4):
+        plane_squares += squares[b]
+    both[core] = plane_squares
+    send(both.at[core], both.at[core], R_SQ + 3, other_core)
+    lax.fori_loop(2, 4, backward_plane, 0)
 
     batch = rewards_ref.shape[1]
     reward = rewards_ref[...].astype(F32)
@@ -439,14 +445,11 @@
     variance = jnp.sum(member * centered * centered, axis=1, keepdims=True) / GROUP
     advantage = (own_reward - mean) / (jnp.sqrt(variance) + 1.0)
 
-    for index, recv in sq_waits:
-        arrive(squares.at[index], recv)
-    clip_squares = jnp.zeros((8, 128), F32)
-    for b in range(8):
-        clip_squares += squares[b]
+    arrive(both.at[1 - core], R_SQ + 3)
+    clip_squares = both[0] + both[1]
     clip_squares = jnp.sum(jnp.sum(clip_squares, axis=1, keepdims=True), axis=0, keepdims=True)
     ratio = jnp.exp(-0.5 * clip_squares / count - one * rollout_ref[x])
-    out_ratio[...] = jnp.broadcast_to(ratio, (8, 128))
+    out_ratio[0] = jnp.sum(ratio)
     low_edge, high_edge = 1.0 - clip_range, 1.0 + clip_range
     inside = (ratio >= low_edge) & (ratio <= high_edge)
     active = inside | ((advantage > 0) & (ratio < low_edge)) | ((advantage < 0) & (ratio > high_edge))
@@ -481,72 +484,76 @@
             send(du.at[where], core_recv, R_RC, other_core)
     arrive(core_recv, R_RC)
     xs[...] = (du[core] + core_recv[...]).astype(BF16)
-    for d in (1, 2, 3):
-        to = (x + d) % 4
-        send(xs.at[rows_at(to * 32, 32, 32), :], xr.at[d - 1], R_RX + d - 1, at(sec, to, z, yl, core))
-    slab = du[core, x_rows, :] + core_recv[x_rows, :]
-    for d in (1, 2, 3):
-        arrive(xr.at[d - 1], R_RX + d - 1)
-        slab += xr[d - 1].astype(F32)
-    zs[...] = slab
-    for d in (1, 2, 3):
-        to = (z + d) % 4
-        send(zs.at[rows_at(to * 8, 8, 8), :], zr.at[d - 1], R_RZ + d - 1, at(sec, x, to, yl, core))
-    z_rows = rows_at(z * 8, 8, 8)
-    piece = zs[z_rows, :]
-    for d in (1, 2, 3):
-        arrive(zr.at[d - 1], R_RZ + d - 1)
-        piece += zr[d - 1]
+
+    def unit(x_, z_):
+        index = x_ * 4 + z_
+        return rows_at((index // 2) * 16, 16, 16), lanes((index % 2) * 512, 512)
+
+    def unit_rows(x_, z_):
+        index = x_ * 4 + z_
+        return index % 2, rows_at((index // 2) * 16, 16, 16)
+
+    for i, (dx, dz) in reversed(list(enumerate(AROUND))):
+        x_, z_ = (x + dx) % 4, (z + dz) % 4
+        rows, cols = unit(x_, z_)
+        send(xs.at[rows, cols], xr.at[i], R_RS + i, at(sec, x_, z_, yl, core))
+    rows, cols = unit(x, z)
+    piece = du[core, rows, cols] + core_recv[rows, cols]
+    for i in range(len(AROUND)):
+        arrive(xr.at[i], R_RS + i)
+        piece += xr[i].astype(F32)
     yr[y] = piece
     for d in (1, 2, 3):
         send(yr.at[y], yr.at[y], R_RY + d - 1, y_peer(d)[1])
     for d in (1, 2, 3):
         arrive(yr.at[(y + 4 - d) % 4], R_RY + d - 1)
-    for b in (0, 1):
-        zg[z_rows, b * 768 : (b + 1) * 768] = yr[2 * b, :, 0:768] + yr[2 * b + 1, :, 0:768]
-        zg[z_rows, HALF + b * 256 : HALF + (b + 1) * 256] = yr[sec * 2 + b, :, 768:1024]
-
-    for d in (1, 2, 3):
-        send(zg.at[z_rows, :], zg.at[z_rows, :], R_GZ + d - 1, at(sec, x, (z + d) % 4, yl, core))
-    for d in (1, 2, 3):
-        arrive(zg.at[rows_at(((z + 4 - d) % 4) * 8, 8, 8), :], R_GZ + d - 1)
-    full[core, x_rows, :] = zg[...].astype(BF16)
-    mine_full = full.at[core, x_rows, :]
-    for d in (1, 2, 3):
-        send(mine_full, mine_full, R_GX + d - 1, at(sec, (x + d) % 4, z, yl, core))
-    send(mine_full, mine_full, R_GC, other_core)
-    for d in (1, 2, 3):
-        from_rows = rows_at(((x + 4 - d) % 4) * 32, 32, 32)
-        arrive(full.at[core, from_rows, :], R_GX + d - 1)
-        send(full.at[core, from_rows, :], full.at[core, from_rows, :], R_GC + d, other_core)
-    for d in (0, 1, 2, 3):
-        from_rows = rows_at(((x + 4 - d) % 4) * 32, 32, 32)
-        arrive(full.at[1 - core, from_rows, :], R_GC + d)
-
-    out_grad[...] = full[...]
+    down_sums = [yr[2 * b] + yr[2 * b + 1] for b in (0, 1)]
+    first_half = jnp.concatenate(down_sums, axis=1)
+    second_half = jnp.concatenate(
+        [part[:, 0:256] for part in down_sums] + [yr[sec * 2 + b, :, 256:512] for b in (0, 1)], axis=1
+    )
+    half, rows = unit_rows(x, z)
+    full[core, half, rows, :] = jnp.where(half == 0, first_half, second_half).astype(BF16)
+
+    own_unit = full.at[core, half, rows, :]
+    for i, (dx, dz) in reversed(list(enumerate(AROUND))):
+        send(own_unit, own_unit, R_AG + i, at(sec, (x + dx) % 4, (z + dz) % 4, yl, core))
+    send(own_unit, own_unit, R_GC + 15, other_core)
+    sources = [unit_rows((x + 4 - dx) % 4, (z + 4 - dz) % 4) for dx, dz in AROUND]
+    for i, (half_, rows_) in enumerate(sources):
+        arrived_unit = full.at[core, half_, rows_, :]
+        arrive(arrived_unit, R_AG + i)
+        send(arrived_unit, arrived_unit, R_GC + i, other_core)
+    for i, (half_, rows_) in enumerate(sources + [(half, rows)]):
+        arrive(full.at[1 - core, half_, rows_, :], R_GC + i)
+
+    load(full, out_grad).wait()
     for copy in pending:
         copy.wait_send()
 
 
 def update(grad_ref, down_ref, up_ref, ratio_ref, out_down, out_up, out_ratio):
     norm_sum = jnp.zeros((128, 256), F32)
-    for b in (0, 1):
-        for j in range(HALF // 256):
-            part = grad_ref[b, :, j * 256 : (j + 1) * 256].astype(F32)
-            norm_sum += part * part
+    for core in (0, 1):
+        for half, width in ((0, 1024), (1, 512)):
+            for j in range(width // 256):
+                part = grad_ref[core, half, :, j * 256 : (j + 1) * 256].astype(F32)
+                norm_sum += part * part
     norm_sum = jnp.sum(jnp.sum(norm_sum, axis=1, keepdims=True), axis=0, keepdims=True)
     factor = step_length / jnp.sqrt(norm_sum * (input_scale * input_scale) + norm_eps)
     down_factor, up_factor = factor * input_scale, factor * out_scale
     for t in range(MODEL_WIDTH // 128):
-        part = grad_ref[(t % 12) // 6, :, (t // 12) * 768 + (t % 6) * 128 : (t // 12) * 768 + (t % 6) * 128 + 128]
+        sec, core, j = t // 12, (t % 12) // 6, t % 6
+        half, start = (0, sec * 512 + j * 128) if j < 4 else (1, sec * 256 + (j - 4) * 128)
+        part = grad_ref[core, half, :, start : start + 128].astype(F32)
         rows = slice(t * 128, (t + 1) * 128)
-        out_down[rows, :] = down_ref[rows, :] - down_factor * jnp.transpose(part.astype(F32))
+        out_down[rows, :] = down_ref[rows, :] - down_factor * jnp.transpose(part)
     for b in (0, 1):
-        for c, width in ((0, 256), (1, 128)):
-            cols = slice(b * OWN + c * 256, b * OWN + c * 256 + width)
-            part = grad_ref[c, :, HALF + b * 256 : HALF + b * 256 + width].astype(F32)
+        for core, width in ((0, 256), (1, 128)):
+            cols = slice(b * OWN + core * 256, b * OWN + core * 256 + width)
+            part = grad_ref[core, 1, :, 512 + b * 256 : 512 + b * 256 + width].astype(F32)
             out_up[:, cols] = up_ref[:, cols] - up_factor * part
-    out_ratio[0] = jnp.sum(ratio_ref[0:1, 0:1])
+    out_ratio[0] = ratio_ref[0]
 
 
 def shards(
@@ -567,7 +574,6 @@
         V((ROWS, MODEL_WIDTH), BF16),
         V((MODEL_WIDTH, 2 * OWN), BF16),
         V((MODEL_WIDTH, 2 * OWN), BF16),
-        V((MODEL_WIDTH, 2 * OWN), BF16),
         V((MODEL_WIDTH, ADAPTER_RANK), BF16),
         V((ADAPTER_RANK, 2 * OWN), BF16),
         V((ROWS, MODEL_WIDTH), F32),
@@ -582,11 +588,14 @@
         V((2 * ROWS, OWN), BF16),
         V((2 * ROWS, ADAPTER_RANK), BF16),
         V((3, 2 * ROWS, 128), F32),
+        V((4, 3, 2 * ROWS, 128), F32),
+        V((4, 3, 2 * ROWS, PLANE), BF16),
         V((3, 2 * ROWS, 128), F32),
         V((2 * ROWS, OWN), F32),
         V((2 * ROWS, OWN), BF16),
         V((4, ROWS, 128), BF16),
-        V((8, 8, 128), F32),
+        V((4, 8, 128), F32),
+        V((2, 8, 128), F32),
         V((2 * ROWS, OWN), BF16),
         V((2 * ROWS, OWN), BF16),
         V((2, ROWS, 128), BF16),
@@ -594,12 +603,9 @@
         V((2, 128, 1024), F32),
         V((128, 1024), F32),
         V((128, 1024), BF16),
-        V((3, 32, 1024), BF16),
-        V((32, 1024), F32),
-        V((3, 8, 1024), F32),
-        V((4, 8, 1024), F32),
-        V((32, 2048), F32),
-        V((2, 128, 2048), BF16),
+        V((15, 16, 512), BF16),
+        V((4, 16, 512), F32),
+        V((2, 2, 128, 1024), BF16),
         pltpu.SemaphoreType.DMA((N_SEND,)),
         pltpu.SemaphoreType.DMA((N_RECV,)),
         pltpu.SemaphoreType.DMA((16,)),
@@ -607,11 +613,11 @@
     gradients, ratio = pl.pallas_call(
         body,
         out_shape=(
-            jax.ShapeDtypeStruct((2, ADAPTER_RANK, 2048), BF16),
-            jax.ShapeDtypeStruct((8, 128), F32),
+            jax.ShapeDtypeStruct((2, 2, ADAPTER_RANK, 1024), BF16),
+            jax.ShapeDtypeStruct((1,), F32),
         ),
         in_specs=[smem] * 3 + [vmem] * 3 + [hbm] * 9,
-        out_specs=(vmem, vmem),
+        out_specs=(hbm, smem),
         scratch_shapes=scratch,
         compiler_params=pltpu.CompilerParams(
             collective_id=0, has_side_effects=True, vmem_limit_bytes=60 * 1024 * 1024
@@ -632,7 +638,7 @@
             jax.ShapeDtypeStruct((ADAPTER_RANK, 2 * OWN), F32),
             jax.ShapeDtypeStruct((1,), F32),
         ),
-        in_specs=[vmem] * 4,
+        in_specs=[vmem] * 3 + [smem],
         out_specs=(vmem, vmem, smem),
         compiler_params=pltpu.CompilerParams(vmem_limit_bytes=32 * 1024 * 1024),
         name="update",

time: 104 us -> 98.2 us (0.944)
  Pallas kernels: 101 us -> 96 us
    pallas_call x1, Pallas kernels: 99.6 us -> 93.7 us  [shards(): pl.pallas_call(body, out_shape=(jax.ShapeDtypeStruct((2, 2, ADAPTER_RANK,...]
where the time goes in v3:
time: 98.2 us; the launch traced here: 98 us
  Pallas kernels  96 us (98%)
  local copies, waits for them, and re-layouts  1.23 us (1%)
    pallas_call x1, Pallas kernels, shards(): pl.pallas_call(body, out_shape=(jax.ShapeDtypeStruct((2, 2, ADAPTER_RANK,...  93.7 us
    pallas_call x1, Pallas kernels, shards(): pl.pallas_call(update, out_shape=(jax.ShapeDtypeStruct((MODEL_WIDTH, ADAP...  2.28 us

profile of v3, /device:TPU:1, one launch (start us, length us, event | category | flops | bytes accessed | tf_op | source)
XLA Modules:
  0.0 98.0 jit_solution(1435042777175055940)
XLA Ops:
  0.6 0.0 copy-start
  0.6 0.0 copy-start.2
  0.7 93.7 %policy_step.1 = (bf16[2,2,128,1024]{3,2,1,0:T(8,128)(2,1)}, f32[1]{0:T(128)}) custom-call(s32[4]{0:T(128)} %chosen_ref.1, s32[4]{0:T(128)} %lengths_ref.1, f32[4]{0:T(128)} %rollout_ref.1, bf16[5,4,32,128]{3,2,1,0:T(8,128)(2,1)} %bitcast.6, s32[1,64]{1,0:T(1,128)} %bitcast.8, s32[1,64]{1,0:T(1,128)} %bitcast.9, f32[4,2,3072]{2,1,0:T(2,128)} %shift_hbm.1, ...), custom_call_target="tpu_custom_call" | custom-call | flops 12000000000 | bytes 24000000 | tf_op jit(solution)/shard_map/policy_step/pallas_call | solution.py:613
  94.4 0.0 copy-done
  94.4 0.0 copy-done.2
  94.4 0.0 copy-start.1
  94.4 1.2 %copy-done.1 = bf16[2,2,128,1024]{3,2,1,0:T(8,128)(2,1)S(1)} copy-done((bf16[2,2,128,1024]{3,2,1,0:T(8,128)(2,1)S(1)}, bf16[2,2,128,1024]{3,2,1,0:T(8,128)(2,1)}, u32[]{:S(2)}) %copy-start.1) | copy-done | bytes 1048600
  95.6 2.3 %update.1 = (f32[3072,128]{1,0:T(8,128)}, f32[128,768]{1,0:T(8,128)}, f32[1]{0:T(128)}) custom-call(bf16[2,2,128,1024]{3,2,1,0:T(8,128)(2,1)S(1)} %copy-done.1, f32[3072,128]{1,0:T(8,128)S(1)} %copy-done, f32[128,768]{1,0:T(8,128)S(1)} %copy-done.2, f32[1]{0:T(128)} %get-tuple-element.6.ratio_ref), custom_call_target="tpu_custom_call" | custom-call | tf_op jit(solution)/shard_map/update/pallas_call | solution.py:634
Async XLA Ops:
  0.6 93.7 %copy-start = (f32[3072,128]{1,0:T(8,128)S(1)}, f32[3072,128]{1,0:T(8,128)}, u32[]{:S(2)}) copy-start(f32[3072,128]{1,0:T(8,128)} %down_ref.1) | copy-start | bytes 4718596
  0.6 93.7 %copy-start.2 = (f32[128,768]{1,0:T(8,128)S(1)}, f32[128,768]{1,0:T(8,128)}, u32[]{:S(2)}) copy-start(f32[128,768]{1,0:T(8,128)} %up_ref.1) | copy-start | bytes 1179652
  94.4 1.2 %copy-start.1 = (bf16[2,2,128,1024]{3,2,1,0:T(8,128)(2,1)S(1)}, bf16[2,2,128,1024]{3,2,1,0:T(8,128)(2,1)}, u32[]{:S(2)}) copy-start(bf16[2,2,128,1024]{3,2,1,0:T(8,128)(2,1)} %get-tuple-element.5.grad_ref) | copy-start | bytes 3145732

commit v4 on v3

--- a/solution.py
+++ b/solution.py
@@ -47,16 +47,14 @@
 R_SQ = 39
 R_LOW = 43
 R_RC = 46
-R_RS = 47
-R_RY = 62
-R_AG = 65
-R_GC = 80
-N_RECV = 96
-N_SEND = 112
-AROUND = sorted(
-    ((dx, dz) for dx in range(4) for dz in range(4) if dx or dz),
-    key=lambda d: min(d[0], 4 - d[0]) + min(d[1], 4 - d[1]),
-)
+R_S1 = 47
+R_S2 = 53
+R_RY = 59
+R_G1 = 62
+R_G2 = 68
+R_GC = 74
+N_RECV = 82
+N_SEND = 96
 
 
 def dot(a, b):
@@ -87,7 +85,7 @@
     shift_ref, patch_ref, wout_ref, down_ref, up_ref, xin, wk, wv, downb, upb, emb, normed,
     sel, latents, stage_k, stage_v, stage_q, keys, values, queries, low,
     top, peaks, probs, total, acc, attn, vel, squares, both, gout, gq, glow_send, glow,
-    du, core_recv, xs, xr, yr, full,
+    du, core_send, core_recv, xs, xr, slabs, slabs_send, zr, yr, full,
     send_sem, recv_sem, local_sem,
 ):
     sec = lax.axis_index("section")
@@ -135,7 +133,8 @@
         return copy
 
 
-    peers = [at(sec, (x + dx) % 4, (z + dz) % 4, yl, core) for dx, dz in AROUND]
+    peers = [at(sec, (x + d) % 4, z, yl, core) for d in (1, 2, 3)]
+    peers += [at(sec, x, (z + d) % 4, yl, core) for d in (1, 2, 3)]
     peers += [y_peer(d)[1] for d in (1, 2, 3)]
     peers += [other_core]
     barrier = pltpu.get_barrier_semaphore()
@@ -167,6 +166,15 @@
     spread = noise_level * jnp.sqrt(step_size * (1.0 - one * chosen.astype(F32) * step_size))
     count = one * (length * PATCH).astype(F32)
 
+    def repeat(stat, count):
+        return jnp.concatenate([stat] * count, axis=1)
+
+    def fold_lanes(op, tile):
+        out = tile[:, 0:128]
+        for j in range(1, tile.shape[1] // 128):
+            out = op(out, tile[:, j * 128 : (j + 1) * 128])
+        return out
+
     expand = jnp.where((iota((ROWS, 128), 0) >> 1) == iota((ROWS, 128), 1), 1.0, 0.0).astype(BF16)
     own_half = (iota((ROWS, 128), 1) >> 6) == (iota((ROWS, 128), 0) & 1)
 
@@ -185,19 +193,20 @@
     now_tokens = dot(token_rows(latents[yl, 0]), fold(0, 64)).astype(BF16)
     for copy in load_x:
         copy.wait()
-    squares_sum = jnp.zeros((ROWS, 1), F32)
+    squares_sum = jnp.zeros((ROWS, 128), F32)
     chunk = 512
     for j in range(MODEL_WIDTH // chunk):
         cols = slice(j * chunk, (j + 1) * chunk)
         part = xin[:, cols].astype(F32) + dot(now_tokens, patch_ref[:, cols])
         emb[:, cols] = part
-        squares_sum += jnp.sum(part * part, axis=1, keepdims=True)
-    inverse = lax.rsqrt(squares_sum * (1.0 / MODEL_WIDTH) + norm_eps)
+        squares_sum += fold_lanes(jnp.add, part * part)
+    mean_square = jnp.sum(squares_sum, axis=1, keepdims=True) * (1.0 / MODEL_WIDTH)
+    inverse = repeat(jnp.broadcast_to(lax.rsqrt(mean_square + norm_eps), (ROWS, 128)), chunk // 128)
     for j in range(MODEL_WIDTH // chunk):
         cols = slice(j * chunk, (j + 1) * chunk)
         shift = shift_ref[chosen, 0:1, cols]
-        scale = shift_ref[chosen, 1:2, cols]
-        normed[:, cols] = (emb[:, cols] * inverse * (1.0 + scale) + shift).astype(BF16)
+        scale = 1.0 + shift_ref[chosen, 1:2, cols]
+        normed[:, cols] = (emb[:, cols] * inverse * scale + shift).astype(BF16)
 
     seq_own = seq * ROWS
     seq_pair = (seq + 2 - 4 * yl) * ROWS
@@ -288,15 +297,6 @@
     def key_bias(start):
         return jnp.where(start + iota((1, PLANE), 1) < length, 0.0, masked_score)
 
-    def repeat(stat, count):
-        return jnp.concatenate([stat] * count, axis=1)
-
-    def fold_lanes(op, tile):
-        out = tile[:, 0:128]
-        for j in range(1, tile.shape[1] // 128):
-            out = op(out, tile[:, j * 128 : (j + 1) * 128])
-        return out
-
     def forward_plane(plane):
         start = ((z + plane) % 4) * PLANE
         plane_rows = rows_at(start, PLANE, PLANE)
@@ -481,51 +481,78 @@
             cols = lanes(sec * HALF + where * 768 + j * 256, 256)
             du[where, :, j * 256 : (j + 1) * 256] = dot(low_turned, normed[:, cols])
         if half == 1:
-            send(du.at[where], core_recv, R_RC, other_core)
+            core_send[...] = du[where].astype(BF16)
+            send(core_send, core_recv, R_RC, other_core)
     arrive(core_recv, R_RC)
-    xs[...] = (du[core] + core_recv[...]).astype(BF16)
-
-    def unit(x_, z_):
-        index = x_ * 4 + z_
-        return rows_at((index // 2) * 16, 16, 16), lanes((index % 2) * 512, 512)
-
-    def unit_rows(x_, z_):
-        index = x_ * 4 + z_
-        return index % 2, rows_at((index // 2) * 16, 16, 16)
-
-    for i, (dx, dz) in reversed(list(enumerate(AROUND))):
-        x_, z_ = (x + dx) % 4, (z + dz) % 4
-        rows, cols = unit(x_, z_)
-        send(xs.at[rows, cols], xr.at[i], R_RS + i, at(sec, x_, z_, yl, core))
-    rows, cols = unit(x, z)
-    piece = du[core, rows, cols] + core_recv[rows, cols]
-    for i in range(len(AROUND)):
-        arrive(xr.at[i], R_RS + i)
-        piece += xr[i].astype(F32)
-    yr[y] = piece
+    summed = du[core] + core_recv[...].astype(F32)
+    du[core] = summed
+    xs[...] = summed.astype(BF16)
+
+    spots = (x, z)
+
+    def along(half, step):
+        if half == 0:
+            other = (x + step) % 4
+            return other, at(sec, other, z, yl, core)
+        other = (z + step) % 4
+        return other, at(sec, x, other, yl, core)
+
+    def slab(index):
+        return rows_at(index * 32, 32, 32)
+
+    def piece_cols(index):
+        return lanes(index * 128, 128)
+
+    for d in (2, 1, 3):
+        for half in (0, 1):
+            other, device = along(half, d)
+            send(xs.at[slab(other), half * 512 : (half + 1) * 512], xr.at[half, d - 1], R_S1 + half * 3 + d - 1, device)
+    for half in (0, 1):
+        part = du[core, slab(spots[half]), half * 512 : (half + 1) * 512]
+        for d in (1, 2, 3):
+            arrive(xr.at[half, d - 1], R_S1 + half * 3 + d - 1)
+            part += xr[half, d - 1].astype(F32)
+        slabs[half] = part
+        slabs_send[half] = part.astype(BF16)
+        for d in (2, 1, 3):
+            other, device = along(1 - half, d)
+            send(slabs_send.at[half, :, piece_cols(other)], zr.at[half, d - 1], R_S2 + half * 3 + d - 1, device)
+    for half in (0, 1):
+        part = slabs[half, :, piece_cols(spots[1 - half])]
+        for d in (1, 2, 3):
+            arrive(zr.at[half, d - 1], R_S2 + half * 3 + d - 1)
+            part += zr[half, d - 1].astype(F32)
+        yr[y, half] = part.astype(BF16)
     for d in (1, 2, 3):
         send(yr.at[y], yr.at[y], R_RY + d - 1, y_peer(d)[1])
     for d in (1, 2, 3):
         arrive(yr.at[(y + 4 - d) % 4], R_RY + d - 1)
-    down_sums = [yr[2 * b] + yr[2 * b + 1] for b in (0, 1)]
-    first_half = jnp.concatenate(down_sums, axis=1)
-    second_half = jnp.concatenate(
-        [part[:, 0:256] for part in down_sums] + [yr[sec * 2 + b, :, 256:512] for b in (0, 1)], axis=1
-    )
-    half, rows = unit_rows(x, z)
-    full[core, half, rows, :] = jnp.where(half == 0, first_half, second_half).astype(BF16)
-
-    own_unit = full.at[core, half, rows, :]
-    for i, (dx, dz) in reversed(list(enumerate(AROUND))):
-        send(own_unit, own_unit, R_AG + i, at(sec, (x + dx) % 4, (z + dz) % 4, yl, core))
-    send(own_unit, own_unit, R_GC + 15, other_core)
-    sources = [unit_rows((x + 4 - dx) % 4, (z + 4 - dz) % 4) for dx, dz in AROUND]
-    for i, (half_, rows_) in enumerate(sources):
-        arrived_unit = full.at[core, half_, rows_, :]
-        arrive(arrived_unit, R_AG + i)
-        send(arrived_unit, arrived_unit, R_GC + i, other_core)
-    for i, (half_, rows_) in enumerate(sources + [(half, rows)]):
-        arrive(full.at[1 - core, half_, rows_, :], R_GC + i)
+    for b in (0, 1):
+        sums = yr[2 * b].astype(F32) + yr[2 * b + 1].astype(F32)
+        full[core, 0, b, slab(x), piece_cols(z)] = sums[0].astype(BF16)
+        full[core, 1, b, slab(z), piece_cols(x)] = jnp.where(x < 2, sums[1], yr[sec * 2 + b, 1].astype(F32)).astype(BF16)
+
+    for d in (2, 1, 3):
+        for half in (0, 1):
+            mine_ = full.at[core, half, :, slab(spots[half]), piece_cols(spots[1 - half])]
+            send(mine_, mine_, R_G1 + half * 3 + d - 1, along(1 - half, d)[1])
+    for half in (0, 1):
+        for d in (1, 2, 3):
+            source = along(1 - half, 4 - d)[0]
+            arrive(full.at[core, half, :, slab(spots[half]), piece_cols(source)], R_G1 + half * 3 + d - 1)
+        mine_ = full.at[core, half, :, slab(spots[half]), :]
+        for d in (2, 1, 3):
+            send(mine_, mine_, R_G2 + half * 3 + d - 1, along(half, d)[1])
+        send(mine_, mine_, R_GC + half * 4, other_core)
+    for d in (1, 3, 2):
+        for half in (0, 1):
+            source = slab(along(half, 4 - d)[0])
+            theirs = full.at[core, half, :, source, :]
+            arrive(theirs, R_G2 + half * 3 + d - 1)
+            send(theirs, theirs, R_GC + half * 4 + d, other_core)
+    for d in (0, 1, 2, 3):
+        for half in (0, 1):
+            arrive(full.at[1 - core, half, :, slab(along(half, 4 - d)[0]), :], R_GC + half * 4 + d)
 
     load(full, out_grad).wait()
     for copy in pending:
@@ -535,23 +562,24 @@
 def update(grad_ref, down_ref, up_ref, ratio_ref, out_down, out_up, out_ratio):
     norm_sum = jnp.zeros((128, 256), F32)
     for core in (0, 1):
-        for half, width in ((0, 1024), (1, 512)):
-            for j in range(width // 256):
-                part = grad_ref[core, half, :, j * 256 : (j + 1) * 256].astype(F32)
-                norm_sum += part * part
+        for sec in (0, 1):
+            for half, width in ((0, 512), (1, 256)):
+                for j in range(width // 256):
+                    part = grad_ref[core, half, sec, :, j * 256 : (j + 1) * 256].astype(F32)
+                    norm_sum += part * part
     norm_sum = jnp.sum(jnp.sum(norm_sum, axis=1, keepdims=True), axis=0, keepdims=True)
     factor = step_length / jnp.sqrt(norm_sum * (input_scale * input_scale) + norm_eps)
     down_factor, up_factor = factor * input_scale, factor * out_scale
     for t in range(MODEL_WIDTH // 128):
         sec, core, j = t // 12, (t % 12) // 6, t % 6
-        half, start = (0, sec * 512 + j * 128) if j < 4 else (1, sec * 256 + (j - 4) * 128)
-        part = grad_ref[core, half, :, start : start + 128].astype(F32)
+        half, start = j // 4, (j % 4) * 128
+        part = grad_ref[core, half, sec, :, start : start + 128].astype(F32)
         rows = slice(t * 128, (t + 1) * 128)
         out_down[rows, :] = down_ref[rows, :] - down_factor * jnp.transpose(part)
     for b in (0, 1):
         for core, width in ((0, 256), (1, 128)):
             cols = slice(b * OWN + core * 256, b * OWN + core * 256 + width)
-            part = grad_ref[core, 1, :, 512 + b * 256 : 512 + b * 256 + width].astype(F32)
+            part = grad_ref[core, 1, b, :, 256 : 256 + width].astype(F32)
             out_up[:, cols] = up_ref[:, cols] - up_factor * part
     out_ratio[0] = ratio_ref[0]
 
@@ -601,11 +629,15 @@
         V((2, ROWS, 128), BF16),
         V((4, ROWS, 128), BF16),
         V((2, 128, 1024), F32),
-        V((128, 1024), F32),
         V((128, 1024), BF16),
-        V((15, 16, 512), BF16),
-        V((4, 16, 512), F32),
-        V((2, 2, 128, 1024), BF16),
+        V((128, 1024), BF16),
+        V((128, 1024), BF16),
+        V((2, 3, 32, 512), BF16),
+        V((2, 32, 512), F32),
+        V((2, 32, 512), BF16),
+        V((2, 3, 32, 128), BF16),
+        V((4, 2, 32, 128), BF16),
+        V((2, 2, 2, 128, 512), BF16),
         pltpu.SemaphoreType.DMA((N_SEND,)),
         pltpu.SemaphoreType.DMA((N_RECV,)),
         pltpu.SemaphoreType.DMA((16,)),
@@ -613,7 +645,7 @@
     gradients, ratio = pl.pallas_call(
         body,
         out_shape=(
-            jax.ShapeDtypeStruct((2, 2, ADAPTER_RANK, 1024), BF16),
+            jax.ShapeDtypeStruct((2, 2, 2, ADAPTER_RANK, 512), BF16),
             jax.ShapeDtypeStruct((1,), F32),
         ),
         in_specs=[smem] * 3 + [vmem] * 3 + [hbm] * 9,

time: 98.2 us -> 97.6 us (level)
  no operation moved by 1% of the time
where the time goes in v4:
time: 97.6 us; the launch traced here: 97.5 us
  Pallas kernels  95.4 us (98%)
  local copies, waits for them, and re-layouts  1.23 us (1%)
    pallas_call x1, Pallas kernels, shards(): pl.pallas_call(body, out_shape=(jax.ShapeDtypeStruct((2, 2, 2, ADAPTER_RA...  93.1 us
    pallas_call x1, Pallas kernels, shards(): pl.pallas_call(update, out_shape=(jax.ShapeDtypeStruct((MODEL_WIDTH, ADAP...  2.28 us

profile of v4, /device:TPU:1, one launch (start us, length us, event | category | flops | bytes accessed | tf_op | source)
XLA Modules:
  0.0 97.5 jit_solution(12714483822454906904)
XLA Ops:
  0.6 0.0 copy-start
  0.6 0.0 copy-start.2
  0.7 93.1 %policy_step.1 = (bf16[2,2,2,128,512]{4,3,2,1,0:T(8,128)(2,1)}, f32[1]{0:T(128)}) custom-call(s32[4]{0:T(128)} %chosen_ref.1, s32[4]{0:T(128)} %lengths_ref.1, f32[4]{0:T(128)} %rollout_ref.1, bf16[5,4,32,128]{3,2,1,0:T(8,128)(2,1)} %bitcast.6, s32[1,64]{1,0:T(1,128)} %bitcast.8, s32[1,64]{1,0:T(1,128)} %bitcast.9, f32[4,2,3072]{2,1,0:T(2,128)} %shift_hbm.1, ...), custom_call_target="tpu_custom_call" | custom-call | flops 12000000000 | bytes 24000000 | tf_op jit(solution)/shard_map/policy_step/pallas_call | solution.py:645
  93.8 0.0 copy-done
  93.8 0.0 copy-done.2
  93.8 0.0 copy-start.1
  93.8 1.2 %copy-done.1 = bf16[2,2,2,128,512]{4,3,2,1,0:T(8,128)(2,1)S(1)} copy-done((bf16[2,2,2,128,512]{4,3,2,1,0:T(8,128)(2,1)S(1)}, bf16[2,2,2,128,512]{4,3,2,1,0:T(8,128)(2,1)}, u32[]{:S(2)}) %copy-start.1) | copy-done | bytes 1048600
  95.0 2.3 %update.1 = (f32[3072,128]{1,0:T(8,128)}, f32[128,768]{1,0:T(8,128)}, f32[1]{0:T(128)}) custom-call(bf16[2,2,2,128,512]{4,3,2,1,0:T(8,128)(2,1)S(1)} %copy-done.1, f32[3072,128]{1,0:T(8,128)S(1)} %copy-done, f32[128,768]{1,0:T(8,128)S(1)} %copy-done.2, f32[1]{0:T(128)} %get-tuple-element.6.ratio_ref), custom_call_target="tpu_custom_call" | custom-call | tf_op jit(solution)/shard_map/update/pallas_call | solution.py:666
Async XLA Ops:
  0.6 93.2 %copy-start = (f32[3072,128]{1,0:T(8,128)S(1)}, f32[3072,128]{1,0:T(8,128)}, u32[]{:S(2)}) copy-start(f32[3072,128]{1,0:T(8,128)} %down_ref.1) | copy-start | bytes 4718596
  0.6 93.2 %copy-start.2 = (f32[128,768]{1,0:T(8,128)S(1)}, f32[128,768]{1,0:T(8,128)}, u32[]{:S(2)}) copy-start(f32[128,768]{1,0:T(8,128)} %up_ref.1) | copy-start | bytes 1179652
  93.8 1.2 %copy-start.1 = (bf16[2,2,2,128,512]{4,3,2,1,0:T(8,128)(2,1)S(1)}, bf16[2,2,2,128,512]{4,3,2,1,0:T(8,128)(2,1)}, u32[]{:S(2)}) copy-start(bf16[2,2,2,128,512]{4,3,2,1,0:T(8,128)(2,1)} %get-tuple-element.5.grad_ref) | copy-start | bytes 3145732

commit v5 on v4

--- a/solution.py
+++ b/solution.py
@@ -238,9 +238,9 @@
         yl_ = yl if pair == 0 else 1 - yl
         send(block(store[kv], z_, yl_, core), block(store[kv], z_, yl_, core), core_index(plane, pair, kv), other_core)
 
-    def from_core(plane):
+    def from_core(plane, pairs=(0, 1)):
         z_ = (z + plane) % 4
-        for pair in (0, 1):
+        for pair in pairs:
             yl_ = yl if pair == 0 else 1 - yl
             for kv in (0, 1):
                 arrive(block(store[kv], z_, yl_, 1 - core), core_index(plane, pair, kv))
@@ -294,13 +294,13 @@
         to_z(1, kv)
         to_core(0, 1, kv)
 
-    def key_bias(start):
-        return jnp.where(start + iota((1, PLANE), 1) < length, 0.0, masked_score)
-
-    def forward_plane(plane):
-        start = ((z + plane) % 4) * PLANE
-        plane_rows = rows_at(start, PLANE, PLANE)
-        bias = key_bias(start)
+    def key_bias(start, width):
+        return jnp.where(start + iota((1, width), 1) < length, 0.0, masked_score)
+
+    def forward_part(plane, slot, offset, width):
+        start = ((z + plane) % 4) * PLANE + offset
+        plane_rows = rows_at(start, width, width)
+        bias = key_bias(start, width)
         first = plane == 0
         tiles = [(h, slice(h * HD, (h + 1) * HD), slice(b * ROWS, (b + 1) * ROWS)) for h in range(3) for b in (0, 1)]
 
@@ -315,17 +315,17 @@
             if not first:
                 before = top[head, rows, :]
                 peak = jnp.maximum(peak, before)
-            exp_scores = jnp.exp2(scores - repeat(peak, PLANE // 128))
+            exp_scores = jnp.exp2(scores - repeat(peak, width // 128))
             sums = fold_lanes(jnp.add, exp_scores)
             kept = exp_scores.astype(BF16)
-            probs[plane, head, rows, :] = kept
+            probs[plane, head, rows, lanes(offset, width)] = kept
             weighted = dot(kept, values[plane_rows, cols])
             if not first:
                 decay = jnp.exp2(before - peak)
                 sums += decay * total[head, rows, :]
                 weighted += decay * acc[rows, cols]
             top[head, rows, :] = peak
-            peaks[plane, head, rows, :] = peak
+            peaks[slot, head, rows, :] = peak
             total[head, rows, :] = sums
             acc[rows, cols] = weighted
 
@@ -340,37 +340,34 @@
             from_z(0, kv, above)
     arrive(queries.at[pair_rows, :], R_PAIR + 2)
     from_core(0)
-    forward_plane(0)
+    forward_part(0, 0, 0, PLANE)
     for kv in (0, 1):
         for above in (0, 1):
             from_z(1, kv, above)
     from_core(1)
-    forward_plane(1)
+    forward_part(1, 1, 0, PLANE)
     from_far(0, 0)
     from_far(0, 1)
     from_core(3)
-    forward_plane(3)
+    forward_part(3, 3, 0, PLANE)
+    from_core(2, (0,))
+    forward_part(2, 2, yl * 512, 512)
     from_far(1, 0)
     from_far(1, 1)
-    from_core(2)
-    forward_plane(2)
-
-    def finish_head(i, carry):
-        head = i // 2
-        cols = lanes(head * HD, HD)
-        rows = rows_at((i % 2) * ROWS, ROWS)
-        sums = jnp.broadcast_to(jnp.sum(total[head, rows, :], axis=1, keepdims=True), (ROWS, 128))
-        attn[rows, cols] = (acc[rows, cols] / sums).astype(BF16)
-        top[head, rows, :] = top[head, rows, :] + jnp.log(sums) * math.log2(math.e)
-        return carry
-
-    lax.fori_loop(0, 6, finish_head, 0)
+    from_core(2, (1,))
+    forward_part(2, 4, (1 - yl) * 512, 512)
+
+    for head in range(3):
+        cols = slice(head * HD, (head + 1) * HD)
+        sums = jnp.broadcast_to(jnp.sum(total[head], axis=1, keepdims=True), (2 * ROWS, 128))
+        attn[:, cols] = (acc[:, cols] / sums).astype(BF16)
+        top[head] = top[head] + jnp.log(sums) * math.log2(math.e)
 
     blank = jnp.zeros((PATCH, OWN), BF16)
     wide = [jnp.concatenate([wout_ref[...], blank], axis=0), jnp.concatenate([blank, wout_ref[...]], axis=0)]
     partial = dot_nt(attn[0:ROWS, :], wide[0]) + dot_nt(attn[ROWS : 2 * ROWS, :], wide[1])
     vel[y] = partial.astype(BF16)
-    for d in (1, 2, 3):
+    for d in (2, 1, 3):
         send(vel.at[y], vel.at[y], R_VEL + d - 1, y_peer(d)[1])
     arrive(latents.at[1 - yl], R_PAIR + 4)
     arrive(low.at[pair_rows, :], R_PAIR + 3)
@@ -404,6 +401,7 @@
 
     def backward_plane(plane, carry):
         plane_rows = rows_at(((z + plane) % 4) * PLANE, PLANE, PLANE)
+        slots = [jnp.where((plane == 2) & (yl == 1 - b), 4, plane) for b in (0, 1)]
 
         def product(head):
             cols = slice(head * HD, (head + 1) * HD)
@@ -411,8 +409,10 @@
 
         def gradient(head, grad_probs):
             cols = slice(head * HD, (head + 1) * HD)
-            scale = jnp.exp2(peaks[plane, head] - top[head])
-            grad_scores = (grad_probs - repeat(total[head], PLANE // 128)) * repeat(scale, PLANE // 128)
+            scale = jnp.concatenate(
+                [repeat(jnp.exp2(peaks[slot, head] - top[head]), 4) for slot in slots], axis=1
+            )
+            grad_scores = (grad_probs - repeat(total[head], PLANE // 128)) * scale
             grad_scores = (probs[plane, head].astype(F32) * grad_scores).astype(BF16)
             acc[:, cols] += dot(grad_scores, keys[plane_rows, cols])
 
@@ -460,7 +460,7 @@
     for b in (0, 1):
         part = dot_nt(gq[b * ROWS : (b + 1) * ROWS, :], upb[:, 0:OWN]) * out_scale
         glow_send[b] = part.astype(BF16)
-    for d in (1, 2, 3):
+    for d in (2, 1, 3):
         other, device = y_peer(d)
         send(glow_send.at[other % 2], glow.at[y], R_LOW + d - 1, device)
     glow[y] = glow_send[yl]
@@ -523,7 +523,7 @@
             arrive(zr.at[half, d - 1], R_S2 + half * 3 + d - 1)
             part += zr[half, d - 1].astype(F32)
         yr[y, half] = part.astype(BF16)
-    for d in (1, 2, 3):
+    for d in (2, 1, 3):
         send(yr.at[y], yr.at[y], R_RY + d - 1, y_peer(d)[1])
     for d in (1, 2, 3):
         arrive(yr.at[(y + 4 - d) % 4], R_RY + d - 1)
@@ -559,17 +559,32 @@
         copy.wait_send()
 
 
-def update(grad_ref, down_ref, up_ref, ratio_ref, out_down, out_up, out_ratio):
+def update(grad_hbm, down_hbm, up_hbm, ratio_ref, out_down, out_up, out_ratio, grad_ref, down_ref, up_ref, sem):
+    copies = {}
+    for core in (0, 1):
+        for half in (0, 1):
+            here = (core, half)
+            copies[here] = pltpu.make_async_copy(grad_hbm.at[here], grad_ref.at[here], sem.at[2 * core + half])
+            copies[here].start()
+    adapters = [
+        pltpu.make_async_copy(down_hbm, down_ref, sem.at[4]),
+        pltpu.make_async_copy(up_hbm, up_ref, sem.at[5]),
+    ]
+    for copy in adapters:
+        copy.start()
     norm_sum = jnp.zeros((128, 256), F32)
     for core in (0, 1):
-        for sec in (0, 1):
-            for half, width in ((0, 512), (1, 256)):
+        for half, width in ((0, 512), (1, 256)):
+            copies[core, half].wait()
+            for sec in (0, 1):
                 for j in range(width // 256):
                     part = grad_ref[core, half, sec, :, j * 256 : (j + 1) * 256].astype(F32)
                     norm_sum += part * part
     norm_sum = jnp.sum(jnp.sum(norm_sum, axis=1, keepdims=True), axis=0, keepdims=True)
     factor = step_length / jnp.sqrt(norm_sum * (input_scale * input_scale) + norm_eps)
     down_factor, up_factor = factor * input_scale, factor * out_scale
+    for copy in adapters:
+        copy.wait()
     for t in range(MODEL_WIDTH // 128):
         sec, core, j = t // 12, (t % 12) // 6, t % 6
         half, start = j // 4, (j % 4) * 128
@@ -616,7 +631,7 @@
         V((2 * ROWS, OWN), BF16),
         V((2 * ROWS, ADAPTER_RANK), BF16),
         V((3, 2 * ROWS, 128), F32),
-        V((4, 3, 2 * ROWS, 128), F32),
+        V((5, 3, 2 * ROWS, 128), F32),
         V((4, 3, 2 * ROWS, PLANE), BF16),
         V((3, 2 * ROWS, 128), F32),
         V((2 * ROWS, OWN), F32),
@@ -670,9 +685,15 @@
             jax.ShapeDtypeStruct((ADAPTER_RANK, 2 * OWN), F32),
             jax.ShapeDtypeStruct((1,), F32),
         ),
-        in_specs=[vmem] * 3 + [smem],
+        in_specs=[hbm] * 3 + [smem],
         out_specs=(vmem, vmem, smem),
-        compiler_params=pltpu.CompilerParams(vmem_limit_bytes=32 * 1024 * 1024),
+        scratch_shapes=[
+            V((2, 2, 2, ADAPTER_RANK, 512), BF16),
+            V((MODEL_WIDTH, ADAPTER_RANK), F32),
+            V((ADAPTER_RANK, 2 * OWN), F32),
+            pltpu.SemaphoreType.DMA((6,)),
+        ],
+        compiler_params=pltpu.CompilerParams(vmem_limit_bytes=61 * 1024 * 1024),
         name="update",
     )(gradients, adapter_down_factor, adapter_up_factor, ratio)
 

time: 97.6 us -> 96.9 us (level)
  local copies, waits for them, and re-layouts: 1.23 us -> 0 us
    pallas_call x1, Pallas kernels: 2.28 us -> 3.95 us  [shards(): pl.pallas_call(update, out_shape=(jax.ShapeDtypeStruct((MODEL_WIDTH, ADAP...]
    unnamed x6 -> x0, local copies, waits for them, and re-layouts: 1.23 us -> none
    pallas_call x1, Pallas kernels: 93.1 us -> 92 us  [shards(): pl.pallas_call(body, out_shape=(jax.ShapeDtypeStruct((2, 2, 2, ADAPTER_RA...]
where the time goes in v5:
time: 96.9 us; the launch traced here: 96.8 us
  Pallas kernels  95.9 us (99%)
    pallas_call x1, Pallas kernels, shards(): pl.pallas_call(body, out_shape=(jax.ShapeDtypeStruct((2, 2, 2, ADAPTER_RA...  92 us
    pallas_call x1, Pallas kernels, shards(): pl.pallas_call(update, out_shape=(jax.ShapeDtypeStruct((MODEL_WIDTH, ADAP...  3.95 us

profile of v5, /device:TPU:1, one launch (start us, length us, event | category | flops | bytes accessed | tf_op | source)
XLA Modules:
  0.0 96.8 jit_solution(15486573397120777136)
XLA Ops:
  0.6 92.0 %policy_step.1 = (bf16[2,2,2,128,512]{4,3,2,1,0:T(8,128)(2,1)}, f32[1]{0:T(128)}) custom-call(s32[4]{0:T(128)} %chosen_ref.1, s32[4]{0:T(128)} %lengths_ref.1, f32[4]{0:T(128)} %rollout_ref.1, bf16[5,4,32,128]{3,2,1,0:T(8,128)(2,1)} %bitcast.6, s32[1,64]{1,0:T(1,128)} %bitcast.8, s32[1,64]{1,0:T(1,128)} %bitcast.9, f32[4,2,3072]{2,1,0:T(2,128)} %shift_hbm.1, ...), custom_call_target="tpu_custom_call" | custom-call | flops 12000000000 | bytes 24000000 | tf_op jit(solution)/shard_map/policy_step/pallas_call | solution.py:660
  92.6 4.0 %update.1 = (f32[3072,128]{1,0:T(8,128)}, f32[128,768]{1,0:T(8,128)}, f32[1]{0:T(128)}) custom-call(bf16[2,2,2,128,512]{4,3,2,1,0:T(8,128)(2,1)} %get-tuple-element.5.grad_hbm, f32[3072,128]{1,0:T(8,128)} %down_hbm.3, f32[128,768]{1,0:T(8,128)} %up_hbm.3, f32[1]{0:T(128)} %get-tuple-element.6.ratio_ref), custom_call_target="tpu_custom_call" | custom-call | tf_op jit(solution)/shard_map/update/pallas_call | solution.py:681

commit v6 on v5

--- a/solution.py
+++ b/solution.py
@@ -550,32 +550,22 @@
             theirs = full.at[core, half, :, source, :]
             arrive(theirs, R_G2 + half * 3 + d - 1)
             send(theirs, theirs, R_GC + half * 4 + d, other_core)
+    handed = [load(full.at[core], out_grad.at[core])]
     for d in (0, 1, 2, 3):
         for half in (0, 1):
             arrive(full.at[1 - core, half, :, slab(along(half, 4 - d)[0]), :], R_GC + half * 4 + d)
-
-    load(full, out_grad).wait()
+    handed.append(load(full.at[1 - core], out_grad.at[1 - core]))
+
+    for copy in handed:
+        copy.wait()
     for copy in pending:
         copy.wait_send()
 
 
-def update(grad_hbm, down_hbm, up_hbm, ratio_ref, out_down, out_up, out_ratio, grad_ref, down_ref, up_ref, sem):
-    copies = {}
-    for core in (0, 1):
-        for half in (0, 1):
-            here = (core, half)
-            copies[here] = pltpu.make_async_copy(grad_hbm.at[here], grad_ref.at[here], sem.at[2 * core + half])
-            copies[here].start()
-    adapters = [
-        pltpu.make_async_copy(down_hbm, down_ref, sem.at[4]),
-        pltpu.make_async_copy(up_hbm, up_ref, sem.at[5]),
-    ]
-    for copy in adapters:
-        copy.start()
+def update(grad_ref, down_ref, up_ref, ratio_ref, out_hbm, out_up, out_ratio, out_down, out_sem):
     norm_sum = jnp.zeros((128, 256), F32)
     for core in (0, 1):
         for half, width in ((0, 512), (1, 256)):
-            copies[core, half].wait()
             for sec in (0, 1):
                 for j in range(width // 256):
                     part = grad_ref[core, half, sec, :, j * 256 : (j + 1) * 256].astype(F32)
@@ -583,20 +573,25 @@
     norm_sum = jnp.sum(jnp.sum(norm_sum, axis=1, keepdims=True), axis=0, keepdims=True)
     factor = step_length / jnp.sqrt(norm_sum * (input_scale * input_scale) + norm_eps)
     down_factor, up_factor = factor * input_scale, factor * out_scale
-    for copy in adapters:
-        copy.wait()
+    written = []
     for t in range(MODEL_WIDTH // 128):
         sec, core, j = t // 12, (t % 12) // 6, t % 6
         half, start = j // 4, (j % 4) * 128
         part = grad_ref[core, half, sec, :, start : start + 128].astype(F32)
         rows = slice(t * 128, (t + 1) * 128)
         out_down[rows, :] = down_ref[rows, :] - down_factor * jnp.transpose(part)
+        if t % 6 == 5:
+            rows = slice((t - 5) * 128, (t + 1) * 128)
+            written.append(pltpu.make_async_copy(out_down.at[rows, :], out_hbm.at[rows, :], out_sem.at[t // 6]))
+            written[-1].start()
     for b in (0, 1):
         for core, width in ((0, 256), (1, 128)):
             cols = slice(b * OWN + core * 256, b * OWN + core * 256 + width)
             part = grad_ref[core, 1, b, :, 256 : 256 + width].astype(F32)
             out_up[:, cols] = up_ref[:, cols] - up_factor * part
     out_ratio[0] = ratio_ref[0]
+    for copy in written:
+        copy.wait()
 
 
 def shards(
@@ -685,15 +680,13 @@
             jax.ShapeDtypeStruct((ADAPTER_RANK, 2 * OWN), F32),
             jax.ShapeDtypeStruct((1,), F32),
         ),
-        in_specs=[hbm] * 3 + [smem],
-        out_specs=(vmem, vmem, smem),
+        in_specs=[vmem] * 3 + [smem],
+        out_specs=(hbm, vmem, smem),
         scratch_shapes=[
-            V((2, 2, 2, ADAPTER_RANK, 512), BF16),
             V((MODEL_WIDTH, ADAPTER_RANK), F32),
-            V((ADAPTER_RANK, 2 * OWN), F32),
-            pltpu.SemaphoreType.DMA((6,)),
+            pltpu.SemaphoreType.DMA((4,)),
         ],
-        compiler_params=pltpu.CompilerParams(vmem_limit_bytes=61 * 1024 * 1024),
+        compiler_params=pltpu.CompilerParams(vmem_limit_bytes=32 * 1024 * 1024),
         name="update",
     )(gradients, adapter_down_factor, adapter_up_factor, ratio)
 

time: 96.9 us -> 97 us (level)
  local copies, waits for them, and re-layouts: 0 us -> 1.23 us
  Pallas kernels: 95.9 us -> 94.7 us
    unnamed x0 -> x6, local copies, waits for them, and re-layouts: none -> 1.23 us
    pallas_call x1, Pallas kernels: 3.95 us -> 2.82 us  [shards(): pl.pallas_call(update, out_shape=(jax.ShapeDtypeStruct((MODEL_WIDTH, ADAP...]
where the time goes in v6:
time: 97 us; the launch traced here: 96.8 us
  Pallas kernels  94.7 us (98%)
  local copies, waits for them, and re-layouts  1.23 us (1%)
    pallas_call x1, Pallas kernels, shards(): pl.pallas_call(body, out_shape=(jax.ShapeDtypeStruct((2, 2, 2, ADAPTER_RA...  91.9 us
    pallas_call x1, Pallas kernels, shards(): pl.pallas_call(update, out_shape=(jax.ShapeDtypeStruct((MODEL_WIDTH, ADAP...  2.82 us

profile of v6, /device:TPU:1, one launch (start us, length us, event | category | flops | bytes accessed | tf_op | source)
XLA Modules:
  0.0 96.8 jit_solution(857424047784926356)
XLA Ops:
  0.6 0.0 copy-start
  0.6 0.0 copy-start.2
  0.7 91.9 %policy_step.1 = (bf16[2,2,2,128,512]{4,3,2,1,0:T(8,128)(2,1)}, f32[1]{0:T(128)}) custom-call(s32[4]{0:T(128)} %chosen_ref.1, s32[4]{0:T(128)} %lengths_ref.1, f32[4]{0:T(128)} %rollout_ref.1, bf16[5,4,32,128]{3,2,1,0:T(8,128)(2,1)} %bitcast.6, s32[1,64]{1,0:T(1,128)} %bitcast.8, s32[1,64]{1,0:T(1,128)} %bitcast.9, f32[4,2,3072]{2,1,0:T(2,128)} %shift_hbm.1, ...), custom_call_target="tpu_custom_call" | custom-call | flops 12000000000 | bytes 24000000 | tf_op jit(solution)/shard_map/policy_step/pallas_call | solution.py:655
  92.6 0.0 copy-done
  92.6 0.0 copy-done.2
  92.6 0.0 copy-start.1
  92.6 1.2 %copy-done.1 = bf16[2,2,2,128,512]{4,3,2,1,0:T(8,128)(2,1)S(1)} copy-done((bf16[2,2,2,128,512]{4,3,2,1,0:T(8,128)(2,1)S(1)}, bf16[2,2,2,128,512]{4,3,2,1,0:T(8,128)(2,1)}, u32[]{:S(2)}) %copy-start.1) | copy-done | bytes 1048600
  93.8 2.8 %update.1 = (f32[3072,128]{1,0:T(8,128)}, f32[128,768]{1,0:T(8,128)}, f32[1]{0:T(128)}) custom-call(bf16[2,2,2,128,512]{4,3,2,1,0:T(8,128)(2,1)S(1)} %copy-done.1, f32[3072,128]{1,0:T(8,128)S(1)} %copy-done, f32[128,768]{1,0:T(8,128)S(1)} %copy-done.2, f32[1]{0:T(128)} %get-tuple-element.6.ratio_ref), custom_call_target="tpu_custom_call" | custom-call | tf_op jit(solution)/shard_map/update/pallas_call | solution.py:676
Async XLA Ops:
  0.6 91.9 %copy-start = (f32[3072,128]{1,0:T(8,128)S(1)}, f32[3072,128]{1,0:T(8,128)}, u32[]{:S(2)}) copy-start(f32[3072,128]{1,0:T(8,128)} %down_ref.1) | copy-start | bytes 4718596
  0.6 91.9 %copy-start.2 = (f32[128,768]{1,0:T(8,128)S(1)}, f32[128,768]{1,0:T(8,128)}, u32[]{:S(2)}) copy-start(f32[128,768]{1,0:T(8,128)} %up_ref.1) | copy-start | bytes 1179652
  92.6 1.2 %copy-start.1 = (bf16[2,2,2,128,512]{4,3,2,1,0:T(8,128)(2,1)S(1)}, bf16[2,2,2,128,512]{4,3,2,1,0:T(8,128)(2,1)}, u32[]{:S(2)}) copy-start(bf16[2,2,2,128,512]{4,3,2,1,0:T(8,128)(2,1)} %get-tuple-element.5.grad_ref) | copy-start | bytes 3145732

commit v7 on v6

--- a/solution.py
+++ b/solution.py
@@ -457,12 +457,12 @@
 
     gq[...] = (acc[...] * (head_scale * weight)).astype(BF16)
 
-    for b in (0, 1):
-        part = dot_nt(gq[b * ROWS : (b + 1) * ROWS, :], upb[:, 0:OWN]) * out_scale
+    for near, steps in ((0, (2,)), (1, (1, 3))):
+        b = (yl + near) % 2
+        part = dot_nt(gq[rows_at(b * ROWS, ROWS), :], upb[:, 0:OWN]) * out_scale
         glow_send[b] = part.astype(BF16)
-    for d in (2, 1, 3):
-        other, device = y_peer(d)
-        send(glow_send.at[other % 2], glow.at[y], R_LOW + d - 1, device)
+        for d in steps:
+            send(glow_send.at[b], glow.at[y], R_LOW + d - 1, y_peer(d)[1])
     glow[y] = glow_send[yl]
     up_part = dot(jnp.transpose(low[...].astype(F32)).astype(BF16), gq[...])
     du[0, :, 768:1024] = up_part[:, 0:256]

time: 97 us -> 97.2 us (level)
  no operation moved by 1% of the time
where the time goes in v7:
time: 97.2 us; the launch traced here: 97 us
  Pallas kernels  94.9 us (98%)
  local copies, waits for them, and re-layouts  1.23 us (1%)
    pallas_call x1, Pallas kernels, shards(): pl.pallas_call(body, out_shape=(jax.ShapeDtypeStruct((2, 2, 2, ADAPTER_RA...  92.1 us
    pallas_call x1, Pallas kernels, shards(): pl.pallas_call(update, out_shape=(jax.ShapeDtypeStruct((MODEL_WIDTH, ADAP...  2.82 us

profile of v7, /device:TPU:1, one launch (start us, length us, event | category | flops | bytes accessed | tf_op | source)
XLA Modules:
  0.0 97.0 jit_solution(16687341946740607882)
XLA Ops:
  0.6 0.0 copy-start
  0.6 0.0 copy-start.2
  0.7 92.1 %policy_step.1 = (bf16[2,2,2,128,512]{4,3,2,1,0:T(8,128)(2,1)}, f32[1]{0:T(128)}) custom-call(s32[4]{0:T(128)} %chosen_ref.1, s32[4]{0:T(128)} %lengths_ref.1, f32[4]{0:T(128)} %rollout_ref.1, bf16[5,4,32,128]{3,2,1,0:T(8,128)(2,1)} %bitcast.6, s32[1,64]{1,0:T(1,128)} %bitcast.8, s32[1,64]{1,0:T(1,128)} %bitcast.9, f32[4,2,3072]{2,1,0:T(2,128)} %shift_hbm.1, ...), custom_call_target="tpu_custom_call" | custom-call | flops 12000000000 | bytes 24000000 | tf_op jit(solution)/shard_map/policy_step/pallas_call | solution.py:655
  92.8 0.0 copy-done
  92.8 0.0 copy-done.2
  92.8 0.0 copy-start.1
  92.8 1.2 %copy-done.1 = bf16[2,2,2,128,512]{4,3,2,1,0:T(8,128)(2,1)S(1)} copy-done((bf16[2,2,2,128,512]{4,3,2,1,0:T(8,128)(2,1)S(1)}, bf16[2,2,2,128,512]{4,3,2,1,0:T(8,128)(2,1)}, u32[]{:S(2)}) %copy-start.1) | copy-done | bytes 1048600
  94.0 2.8 %update.1 = (f32[3072,128]{1,0:T(8,128)}, f32[128,768]{1,0:T(8,128)}, f32[1]{0:T(128)}) custom-call(bf16[2,2,2,128,512]{4,3,2,1,0:T(8,128)(2,1)S(1)} %copy-done.1, f32[3072,128]{1,0:T(8,128)S(1)} %copy-done, f32[128,768]{1,0:T(8,128)S(1)} %copy-done.2, f32[1]{0:T(128)} %get-tuple-element.6.ratio_ref), custom_call_target="tpu_custom_call" | custom-call | tf_op jit(solution)/shard_map/update/pallas_call | solution.py:676
Async XLA Ops:
  0.6 92.1 %copy-start = (f32[3072,128]{1,0:T(8,128)S(1)}, f32[3072,128]{1,0:T(8,128)}, u32[]{:S(2)}) copy-start(f32[3072,128]{1,0:T(8,128)} %down_ref.1) | copy-start | bytes 4718596
  0.6 92.1 %copy-start.2 = (f32[128,768]{1,0:T(8,128)S(1)}, f32[128,768]{1,0:T(8,128)}, u32[]{:S(2)}) copy-start(f32[128,768]{1,0:T(8,128)} %up_ref.1) | copy-start | bytes 1179652
  92.8 1.2 %copy-start.1 = (bf16[2,2,2,128,512]{4,3,2,1,0:T(8,128)(2,1)S(1)}, bf16[2,2,2,128,512]{4,3,2,1,0:T(8,128)(2,1)}, u32[]{:S(2)}) copy-start(bf16[2,2,2,128,512]{4,3,2,1,0:T(8,128)(2,1)} %get-tuple-element.5.grad_ref) | copy-start | bytes 3145732
